TPU v7x, 512 devices: a whole 4x8x8 slice. The times are simulated.
512 devices in a mesh: tm: 16 (over z, core), chan: 32 (over y, x).
Axes of the slice: x: 4, y: 8, z: 8, core: 2. Of those that a mesh axis runs over, the one named last changes fastest.
Arguments:
- raw: bfloat16 [65536, 8192], P('chan', 'tm'), may hold values from -6 to 6
- band_taps: float32 [3, 257], replicated, may hold values from -0.375 to 0.375
- band_gain: float32 [16], replicated, may hold values from 0.25 to 4
- gain_index: int32 [65536, 3], P('chan'), may hold values from 0 to 15
- owner_of: int32 [65536, 1], replicated, may hold values from 0 to 31; in each aligned block of 128 rows (0 to 127, 128 to 255, ...) at most 8 rows name the same one
- seat: int32 [65536], replicated, may hold values from 0 to 4
- cable_length: int32 [160], P('chan'), may hold values from 8 to 63
Outputs:
- cable_series: float32 [160, 8192], P('chan', 'tm')
Inputs may be any that keep to these rules, and one draw needn't show every extreme that they name: `owner_of`: among the channels of one device (aligned blocks of 128 channel numbers c = (j * 16 + t) * 128 + i), at most 8 have one owner, and some owner has exactly 8; every owner is used.
All inputs are finite; a program needn't handle non-finite values.
Results may differ from a plain program's by a relative error of at most 0.0066.
Values may be sent and summed in bfloat16 or wider, within the bound.
No kernel may reach another device: no remote copies, remote signals or barrier semaphores. Data moves between devices by JAX's collectives and lax.ppermute only.
A program may use at most 128 MiB of HBM per device.

v0:
```python
import jax
import jax.numpy as jnp
from jax import lax
from jax.sharding import PartitionSpec as P


def make_matrix(band_taps):
    tap_values = band_taps.astype(jnp.bfloat16)
    bands_count, width = tap_values.shape
    half_width = width // 2
    tile_len = 2 * half_width
    period = 3 * tile_len + 1
    padded_taps = jnp.pad(tap_values, ((0, 0), (0, period - width)))
    tiled = jnp.tile(padded_taps, (1, 2 * tile_len))[:, : 2 * tile_len * (period - 1)]
    toeplitz = tiled.reshape(bands_count, 2 * tile_len, period - 1)[:, :, tile_len : 2 * tile_len]
    return (
        jnp.transpose(toeplitz, (1, 0, 2)).reshape(2 * tile_len, bands_count * tile_len),
        half_width,
    )


def filter_rows(rows, band_taps, gain_rows):
    band_matrix, half_width = make_matrix(band_taps)
    tile_len = 2 * half_width
    chan_dev, samples = rows.shape
    tile_count = -(-samples // tile_len)
    padded_len = tile_count * tile_len
    padded = jnp.pad(rows, ((0, 0), (half_width, half_width + padded_len - samples)))
    middle = padded[:, half_width : half_width + padded_len].reshape(chan_dev, tile_count, tile_len)
    behind = padded[:, :padded_len].reshape(chan_dev, tile_count, tile_len)[:, :, :half_width]
    ahead_part = padded[:, tile_len : tile_len + padded_len].reshape(
        chan_dev, tile_count, tile_len
    )[:, :, half_width:]
    windowed = jnp.concatenate((behind, middle, ahead_part), axis=2)
    band_out = jnp.einsum("cnj,jm->cnm", windowed, band_matrix, preferred_element_type=jnp.float32)
    band_out = band_out.reshape(chan_dev, tile_count, 3, tile_len)
    filtered = (
        gain_rows[:, 0, None, None] * band_out[:, :, 0]
        + gain_rows[:, 1, None, None] * band_out[:, :, 1]
        + gain_rows[:, 2, None, None] * band_out[:, :, 2]
    )
    filtered = filtered.reshape(chan_dev, padded_len)
    padded_edges = jnp.pad(filtered, ((0, 0), (1, 1)))
    return (0.5 * (padded_edges[:, 2:] - padded_edges[:, :-2])).astype(jnp.bfloat16)


def signed_power(rate_rows):
    values = rate_rows.astype(jnp.float32)
    return values * jnp.abs(values)


def earlier_count(flags, axis_len):
    lower = (jnp.arange(axis_len)[:, None] > jnp.arange(axis_len)[None, :]).astype(jnp.float32)
    return (lower, flags.astype(jnp.float32))


def shards(raw, band_taps, band_gain, gain_index, owner_of, seat, cable_length):
    tm_count = lax.axis_size("tm")
    chan_count = lax.axis_size("chan")
    tm_pos = lax.axis_index("tm")
    chan_pos = lax.axis_index("chan")
    group_len, samples_dev = raw.shape
    chan_dev = group_len // tm_count
    samples = samples_dev * tm_count
    pieces = raw.reshape(tm_count, chan_dev, samples_dev)
    regrouped = lax.all_to_all(pieces, "tm", split_axis=0, concat_axis=2, tiled=True)[0]
    my_index = lax.dynamic_slice_in_dim(gain_index, tm_pos * chan_dev, chan_dev, 0)
    levels = band_gain.shape[0]
    gain_rows = jnp.sum(
        jnp.where(
            my_index[:, :, None] == jnp.arange(levels)[None, None, :], band_gain[None, None, :], 0.0
        ),
        axis=2,
    )
    strain_rate = filter_rows(regrouped, band_taps, gain_rows)
    owners = owner_of[:, 0]
    channel_start = chan_pos * group_len + tm_pos * chan_dev
    my_owner = lax.dynamic_slice_in_dim(owners, channel_start, chan_dev, 0)
    cab_dev = cable_length.shape[0]
    capacity = 2 * chan_dev // chan_count
    owner_hits = (my_owner[:, None] == jnp.arange(chan_count)[None, :]).astype(jnp.int32)
    lower, hit_values = earlier_count(owner_hits, chan_dev)
    before_count = jnp.dot(lower, hit_values, precision=lax.Precision.HIGHEST).astype(jnp.int32)
    slot_rank = jnp.sum(before_count * owner_hits, axis=1)
    slot_index = my_owner * capacity + slot_rank
    selector = (jnp.arange(chan_count * capacity)[:, None] == slot_index[None, :]).astype(
        jnp.bfloat16
    )
    outgoing = jnp.dot(selector, strain_rate, preferred_element_type=jnp.float32).astype(
        jnp.bfloat16
    )
    outgoing = outgoing.reshape(chan_count, capacity, samples)
    incoming = lax.all_to_all(outgoing, "chan", split_axis=0, concat_axis=0, tiled=True)
    source_owner = lax.dynamic_index_in_dim(
        owners.reshape(chan_count, tm_count, chan_dev), tm_pos, 1, keepdims=False
    )
    source_seat = lax.dynamic_index_in_dim(
        seat.reshape(chan_count, tm_count, chan_dev), tm_pos, 1, keepdims=False
    )
    from_here = (source_owner == chan_pos).astype(jnp.int32)
    lower_rows, here_values = earlier_count(from_here, chan_dev)
    arrival = jnp.dot(here_values, lower_rows.T, precision=lax.Precision.HIGHEST).astype(jnp.int32)
    at_slot = (
        (arrival[:, :, None] == jnp.arange(capacity)[None, None, :]) & (from_here[:, :, None] > 0)
    ).astype(jnp.float32)
    at_cable = (source_seat[:, :, None] == jnp.arange(cab_dev)[None, None, :]).astype(jnp.float32)
    weights = jnp.einsum("sic,sik->ksc", at_slot, at_cable, precision=lax.Precision.HIGHEST)
    weights = weights.reshape(cab_dev, chan_count * capacity)
    arrived_power = signed_power(incoming.reshape(chan_count * capacity, samples))
    partial_value = jnp.dot(weights, arrived_power, precision=lax.Precision.HIGHEST)
    summed = lax.psum_scatter(partial_value, "tm", scatter_dimension=1, tiled=True)
    return summed / cable_length.astype(jnp.float32)[:, None]


def solution(mesh):
    return jax.shard_map(
        shards,
        mesh=mesh,
        in_specs=(P("chan", "tm"), P(), P(), P("chan", None), P(), P(), P("chan")),
        out_specs=P("chan", "tm"),
        check_vma=False,
    )
```

profile of v0, /device:TPU:4, one launch (start us, length us, event | category | flops | bytes accessed | tf_op | source)
XLA Modules:
  0.0 301.4 jit_solution(7004662143526515806)
XLA Ops:
  6.5 10.6 %all-to-all-start = ((bf16[16,128,512]{2,1,0:T(8,128)(2,1)}), bf16[16,128,512]{2,1,0:T(8,128)(2,1)}, u32[]{:S(2)}, u32[]{:S(2)}) async-start(bf16[16,128,512]{2,1,0:T(8,128)(2,1)} %bitcast.74), calls=%async_computation | async-start | bytes 4194304 | tf_op jit(solution)/shard_map/all_to_all | solution.py:66
  17.2 0.2 tile.4
  17.4 5.8 %reshape.83 = bf16[1181184]{0:T(1024)(128)(2,1)} reshape(bf16[3,512,769]{2,1,0:T(8,128)(2,1)S(1)} %tile.4) | data formatting | bytes 4724736
  23.2 2.9 tile.10
  26.1 1.1 slice.59
  27.3 0.3 copy.70
  27.7 1.2 copy.59
  28.9 0.7 fusion.22
  29.5 0.7 constant_dynamic-slice_fusion
  30.2 0.2 fusion.11
  30.5 0.7 multiply_add_fusion
  31.2 35.2 %all-to-all-done = bf16[16,128,512]{2,1,0:T(8,128)(2,1)} async-done(((bf16[16,128,512]{2,1,0:T(8,128)(2,1)}), bf16[16,128,512]{2,1,0:T(8,128)(2,1)}, u32[]{:S(2)}, u32[]{:S(2)}) %all-to-all-start) | async-done | bytes 2097184 | tf_op jit(solution)/shard_map/all_to_all | solution.py:66
  66.4 3.0 %copy.54 = bf16[1,128,16,512]{1,3,2,0:T(8,128)(2,1)S(1)} copy(bf16[1,128,16,512]{3,1,2,0:T(8,128)(2,1)} %bitcast.9) | data formatting | bytes 4194304 | tf_op jit(solution)/shard_map/all_to_all | solution.py:66
  69.4 1.6 pad_slice_fusion.1
  71.1 1.3 copy.65
  72.4 1.3 slice.58
  73.7 1.3 copy.66
  75.1 2.9 copy.58
  78.0 10.1 %fusion.2 = f32[128,32,3,256]{3,0,2,1:T(8,128)} fusion(bf16[128,32,128]{2,0,1:T(8,128)(2,1)} %copy.66, bf16[128,32,256]{2,0,1:T(8,128)(2,1)} %copy.58, bf16[128,32,128]{2,0,1:T(8,128)(2,1)S(1)} %copy-done.1, bf16[512,3,256]{0,2,1:T(8,128)(2,1)} %copy.59), kind=kOutput, calls=%fused_computation.6 | convolution fusion | flops 3233808384 | bytes 17563648 | tf_op jit(solution)/shard_map/cnj,jm->cnm/dot_general | solution.py:35
  88.1 9.6 %fusion.27 = (f32[128,32,1,256]{3,0,2,1:T(8,128)}, f32[128,32,1,256]{3,0,2,1:T(8,128)}, f32[128,32,1,256]{3,0,2,1:T(8,128)}) fusion(f32[128,32,3,256]{3,0,2,1:T(8,128)} %fusion.2), kind=kLoop, calls=%fused_computation.59 | loop fusion | bytes 25165824 | tf_op jit(solution)/shard_map/slice | solution.py:38
  97.6 5.6 %copy.60 = f32[128,32,1,256]{0,3,1,2:T(8,128)} copy(f32[128,32,1,256]{3,0,2,1:T(8,128)} %get-tuple-element.5) | data formatting | bytes 8388608 | tf_op jit(solution)/shard_map/slice | solution.py:38
  103.2 5.6 %copy.61 = f32[128,32,1,256]{0,3,1,2:T(8,128)} copy(f32[128,32,1,256]{3,0,2,1:T(8,128)} %get-tuple-element.7) | data formatting | bytes 8388608 | tf_op jit(solution)/shard_map/slice | solution.py:39
  108.8 5.6 %copy.62 = f32[128,32,1,256]{0,3,1,2:T(8,128)} copy(f32[128,32,1,256]{3,0,2,1:T(8,128)} %get-tuple-element.6) | data formatting | bytes 8388608 | tf_op jit(solution)/shard_map/slice | solution.py:40
  114.4 5.3 %fusion.7 = f32[128,8192]{0,1:T(8,128)S(1)} fusion(f32[128,32,1,256]{0,3,1,2:T(8,128)} %copy.62, f32[128,32,1,256]{0,3,1,2:T(8,128)} %copy.61, f32[128,32,1,256]{0,3,1,2:T(8,128)} %copy.60, f32[128]{0:T(128)S(1)} %get-tuple-element.13, f32[128]{0:T(128)S(1)} %get-tuple-element.14, f32[128]{0:T(128)S(1)} %get-tuple-element.12), kind=kLoop, calls=%fused_computation.12 | loop fusion | flops 5242880 | bytes 16778752 | tf_op jit(solution)/shard_map/add | solution.py:38
  119.7 3.3 %fusion = bf16[32,8,8192]{2,1,0:T(8,128)(2,1)} fusion(f32[128,8192]{0,1:T(8,128)S(1)} %fusion.7, s32[128]{0:T(128)S(1)} %multiply_add_fusion), kind=kOutput, calls=%fused_computation.2 | convolution fusion | flops 542146560 | bytes 8389120 | tf_op jit(solution)/shard_map/dot_general | solution.py:89
  123.0 10.3 %all-to-all-start.1 = ((bf16[32,8,8192]{2,1,0:T(8,128)(2,1)}), bf16[32,8,8192]{2,1,0:T(8,128)(2,1)}, u32[]{:S(2)}, u32[]{:S(2)}) async-start(bf16[32,8,8192]{2,1,0:T(8,128)(2,1)} %fusion), calls=%async_computation.1 | async-start | bytes 8388608 | tf_op jit(solution)/shard_map/all_to_all | solution.py:93
  133.4 0.9 broadcast_compare_fusion
  134.6 0.2 convolution_bitcast_fusion.1
  134.8 91.8 %all-to-all-done.1 = bf16[32,8,8192]{2,1,0:T(8,128)(2,1)} async-done(((bf16[32,8,8192]{2,1,0:T(8,128)(2,1)}), bf16[32,8,8192]{2,1,0:T(8,128)(2,1)}, u32[]{:S(2)}, u32[]{:S(2)}) %all-to-all-start.1) | async-done | bytes 4194336 | tf_op jit(solution)/shard_map/all_to_all | solution.py:93
  226.6 9.5 %convolution_bitcast_fusion = f32[5,8192]{1,0:T(8,128)} fusion(f32[5,32,8]{2,0,1:T(8,128)S(1)} %convolution_bitcast_fusion.1, bf16[32,8,8192]{2,1,0:T(8,128)(2,1)} %all-to-all-done.1), kind=kOutput, calls=%fused_computation.3 | convolution fusion | flops 132120576 | bytes 4363264 | tf_op jit(solution)/shard_map/dot_general | solution.py:110
  236.1 57.1 %reduce-scatter.2.cloned.1.call-done = f32[5,512]{1,0:T(8,128)} async-done(((f32[5,8192]{1,0:T(8,128)}), f32[5,512]{1,0:T(8,128)}) %reduce-scatter.2.cloned.1.call-update) | async-done | bytes 10256 | tf_op jit(solution)/shard_map/reduce_scatter | solution.py:111
  293.2 1.4 broadcast_divide_fusion
  (22 shorter events, 0.5 us)
Async XLA Ops:
  6.5 127.8 %copy-start = (s32[65536]{0:T(1024)S(1)}, s32[65536]{0:T(1024)}, u32[]{:S(2)}) copy-start(s32[65536]{0:T(1024)} %param.12) | copy-start | bytes 786436
  6.5 10.6 %copy-start.2 = (f32[3,257]{1,0:T(4,128)S(1)}, f32[3,257]{1,0:T(4,128)}, u32[]{:S(2)}) copy-start(f32[3,257]{1,0:T(4,128)} %param.8) | copy-start | bytes 9256
  6.5 59.8 %all-to-all-start = ((bf16[16,128,512]{2,1,0:T(8,128)(2,1)}), bf16[16,128,512]{2,1,0:T(8,128)(2,1)}, u32[]{:S(2)}, u32[]{:S(2)}) async-start(bf16[16,128,512]{2,1,0:T(8,128)(2,1)} %bitcast.74), calls=%async_computation | async-start | bytes 4194304 | tf_op jit(solution)/shard_map/all_to_all | solution.py:66
  27.3 3.1 %copy-start.3 = (f32[16]{0:T(128)S(1)}, f32[16]{0:T(128)}, u32[]{:S(2)}) copy-start(f32[16]{0:T(128)} %param.9) | copy-start | bytes 196
  75.1 2.9 copy-start.1
  123.0 103.5 %all-to-all-start.1 = ((bf16[32,8,8192]{2,1,0:T(8,128)(2,1)}), bf16[32,8,8192]{2,1,0:T(8,128)(2,1)}, u32[]{:S(2)}, u32[]{:S(2)}) async-start(bf16[32,8,8192]{2,1,0:T(8,128)(2,1)} %fusion), calls=%async_computation.1 | async-start | bytes 8388608 | tf_op jit(solution)/shard_map/all_to_all | solution.py:93
  133.3 159.9 %reduce-scatter.2.cloned.1.call-start = ((), (), s32[]{:S(2)}) async-start(), calls=%async_computation.3 | async-start | bytes 278528 | tf_op jit(solution)/shard_map/reduce_scatter | solution.py:111
  134.3 101.8 %copy-start.4 = (s32[5]{0:T(128)S(1)}, s32[5]{0:T(128)}, u32[]{:S(2)}) copy-start(s32[5]{0:T(128)} %param.13) | copy-start | bytes 64
Sparse Core Ops, SparseCore 0:
  236.2 56.9 reduce-scatter.1
where the time goes:
time: 302 us; the launch traced here: 301 us
  waiting for transfers between devices  184 us (61%)
  local copies, waits for them, and re-layouts  50.9 us (17%)
  matrix products  23.5 us (8%)
  starting transfers between devices  20.9 us (7%)
  between operations  13.6 us (5%)
  other arithmetic  8.44 us (3%)
    all_to_all x1, waiting for transfers between devices, shards(): lax.all_to_all(outgoing, 'chan', split_axis=0, concat_axis=0, tiled=True)  91.8 us
    reduce_scatter x1, waiting for transfers between devices, shards(): lax.psum_scatter(partial_value, 'tm', scatter_dimension=1, tiled=True)  57.1 us
    all_to_all x1, waiting for transfers between devices, shards(): lax.all_to_all(pieces, 'tm', split_axis=0, concat_axis=2, tiled=True)[0]  35.2 us
    slice x2, local copies, waits for them, and re-layouts, filter_rows(): band_out[:, :, 0]  15.1 us
    all_to_all x1, starting transfers between devices, shards(): lax.all_to_all(pieces, 'tm', split_axis=0, concat_axis=2, tiled=True)[0]  10.6 us
    all_to_all x1, starting transfers between devices, shards(): lax.all_to_all(outgoing, 'chan', split_axis=0, concat_axis=0, tiled=True)  10.3 us
    dot_general x1, matrix products, filter_rows(): jnp.einsum('cnj,jm->cnm', windowed, band_matrix, preferred_element_type=j...  10.1 us
    dot_general x1, matrix products, shards(): jnp.dot(weights, arrived_power, precision=lax.Precision.HIGHEST)  9.54 us
  transfers between devices with their start and end apart: 3, of which 3 were waited for; matrix products, arithmetic and copies ran while one was open for 5% of the time, Pallas kernels for 0%

commit v1 on v0

v1 whole, which is shorter than its diff:
```python
import functools

import jax
import jax.numpy as jnp
from jax import lax
from jax.experimental import pallas as pl
from jax.experimental.pallas import tpu as pltpu
from jax.sharding import PartitionSpec as P

LANES = 128
SIDE = 144
INNER = 256
SIDE_COLS = 2048
INNER_COLS = 2048
F32 = jnp.float32
BF16 = jnp.bfloat16
NT = (((1,), (1,)), ((), ()))


def beside_rows(beside, lane_at):
    count = beside.shape[0]
    lane = lax.broadcasted_iota(jnp.int32, (16, LANES), 1)
    pick = (lane == lane_at).astype(F32).astype(BF16)
    column = lax.dot_general(pick, beside, NT, preferred_element_type=F32)
    rows = [column[0:1, a * LANES : (a + 1) * LANES] for a in range(count // LANES)]
    return jnp.concatenate(rows, axis=0).astype(BF16)


def is_low_core():
    return lax.axis_index("tm") % 2 == 0


def pack_kernel(is_far, raw_ref, *refs):
    strip_ref = refs[-1]
    count = raw_ref.shape[0]
    core = lax.axis_index("tm") % 2
    side = core if is_far else 1 - core
    strip_ref[0:count, :] = raw_ref[:, pl.ds(pl.multiple_of(side * (3 * LANES), LANES), LANES)]
    beside = raw_ref[:, pl.ds(pl.multiple_of(LANES + side * LANES, LANES), LANES)]
    strip_ref[count:, :] = beside_rows(beside, side * (LANES - 1))


def pack(raw, is_far, *after):
    count, depth = raw.shape
    vmem = pl.BlockSpec(memory_space=pltpu.VMEM)
    return pl.pallas_call(
        functools.partial(pack_kernel, is_far),
        in_specs=[vmem] + [pl.BlockSpec(memory_space=pl.ANY)] * len(after),
        out_specs=vmem,
        out_shape=jax.ShapeDtypeStruct((count + 16, LANES), BF16),
        compiler_params=pltpu.CompilerParams(vmem_limit_bytes=8 << 20),
        cost_estimate=pl.CostEstimate(
            flops=2 * count * depth * 768, bytes_accessed=4 << 20, transcendentals=0
        ),
        name="far_strip" if is_far else "near_strip",
    )(raw, *after)


def window_sums(columns_of, taps_ref, size, gains_ref, edges_of, onehot_ref, count, step):
    sub = lax.broadcasted_iota(jnp.int32, (8, step), 0)
    total = None
    for start in range(0, count, step):
        part = slice(start, start + step)
        bands = lax.dot_general(taps_ref[...], columns_of(part), NT, preferred_element_type=F32)
        held = gains_ref[0:1, part] * bands[0:size]
        for b in (1, 2):
            held = held + gains_ref[b : b + 1, part] * bands[b * size : (b + 1) * size]
        first, last = held[0:8], held[size - 8 : size]
        if edges_of is not None:
            low, high = edges_of(start)
            first = first + jnp.where(sub == 0, low, 0.0)
            last = last + jnp.where(sub == 7, high, 0.0)
        middle = held[8 : size - 8]
        ahead = jnp.concatenate([middle, last, pltpu.roll(first, 7, 0)], axis=0)
        behind = jnp.concatenate([pltpu.roll(last, 1, 0), first, middle], axis=0)
        rate = (ahead - behind).astype(BF16)
        power = rate * jnp.abs(rate)
        term = lax.dot_general(onehot_ref[:, part], power, NT, preferred_element_type=F32)
        total = term if total is None else total + term
    return total


def sample_of_row(rows, size, cols):
    row = lax.broadcasted_iota(jnp.int32, (rows, cols), 0)
    return jnp.bitwise_and(row, 7) * (size // 8) + jnp.right_shift(row, 3)


def prepare_kernel(
    levels_ref, taps_ref, index_ref, place_ref,
    inner_taps_ref, far_taps_ref, near_taps_ref, gains_ref, onehot_ref,
):
    is_low = is_low_core()
    tm_pos = lax.axis_index("tm")
    inside = jnp.logical_and(tm_pos > 0, tm_pos < lax.axis_size("tm") - 1).astype(F32)
    count = index_ref.shape[1]
    depth = inner_taps_ref.shape[1]
    bands, width = taps_ref.shape
    blocks = count // LANES
    wide = depth + LANES

    reach = 3 * LANES
    lane = lax.broadcasted_iota(jnp.int32, (bands, reach - 2 * LANES), 1)
    tail = jnp.where(lane == 0, taps_ref[:, width - 1 : width], 0.0)
    taps = jnp.concatenate([taps_ref[:, 0 : width - 1], tail], axis=1).astype(BF16)
    turn = (
        lax.broadcasted_iota(jnp.int32, (reach, wide), 0) + lax.broadcasted_iota(jnp.int32, (reach, wide), 1)
        == width - 1
    )
    base = jnp.dot(taps, turn.astype(F32).astype(BF16), preferred_element_type=F32)
    sub = lax.broadcasted_iota(jnp.int32, (8, depth), 0)

    row = lax.broadcasted_iota(jnp.int32, (8, wide), 0)

    def rows_of(b, size, shifts):
        line = jnp.broadcast_to(base[b : b + 1, :], (8, wide))
        spread = size // 8
        fan = line
        for i in range(1, 8):
            fan = jnp.where(row == i, pltpu.roll(line, i * spread, 1), fan)
        return [
            [pltpu.roll(fan, (j + shift) % wide, 1)[:, 0:depth] for j in range(spread)]
            for shift in shifts
        ]

    for b in range(bands):
        (rows,) = rows_of(b, INNER, (0,))
        for j in range(0, INNER // 8, 2):
            at = b * INNER + 8 * j
            inner_taps_ref[at : at + 16, :] = jnp.concatenate(rows[j : j + 2], axis=0).astype(BF16)
        low, high = rows_of(b, SIDE, (-1, 2 * LANES + 1 - SIDE))
        low[0] = jnp.where(sub == 0, low[0] * jnp.where(is_low, inside, 1.0), low[0])
        high[-1] = jnp.where(sub == 7, high[-1] * jnp.where(is_low, 1.0, inside), high[-1])
        for j in range(0, SIDE // 8, 2):
            at = slice(b * SIDE + 8 * j, b * SIDE + 8 * j + 16)
            low_rows = jnp.concatenate(low[j : j + 2], axis=0).astype(BF16)
            high_rows = jnp.concatenate(high[j : j + 2], axis=0).astype(BF16)
            high_rows = jnp.concatenate([high_rows[:, 3 * LANES :], high_rows[:, : 3 * LANES]], axis=1)

            @pl.when(is_low)
            def _():
                far_taps_ref[at, :] = low_rows
                near_taps_ref[at, :] = high_rows

            @pl.when(jnp.logical_not(is_low))
            def _():
                far_taps_ref[at, :] = high_rows
                near_taps_ref[at, :] = low_rows

    index = index_ref[...]
    gains = jnp.zeros(index.shape, F32)
    for level in range(levels_ref.shape[0]):
        gains = jnp.where(index == level, levels_ref[level], gains)
    gains = 0.5 * gains
    first = taps_ref[:, 0:1].astype(BF16).astype(F32)
    final = taps_ref[:, width - 1 : width].astype(BF16).astype(F32)
    low_edge = jnp.sum(gains * final, axis=0, keepdims=True)
    high_edge = jnp.sum(gains * first, axis=0, keepdims=True)
    gains_ref[0:bands, :] = gains
    gains_ref[3:4, :] = jnp.where(is_low, low_edge, high_edge)
    gains_ref[4:5, :] = jnp.where(is_low, high_edge, low_edge)
    place = place_ref[...]
    cable = lax.broadcasted_iota(jnp.int32, (onehot_ref.shape[0], LANES), 0)
    for a in range(blocks):
        onehot_ref[:, a * LANES : (a + 1) * LANES] = (cable == place[a : a + 1, :]).astype(F32).astype(BF16)


def prepare(band_gain, taps, index, place, cables, depth):
    count = index.shape[1]
    bands = taps.shape[0]
    smem = pl.BlockSpec(memory_space=pltpu.SMEM)
    vmem = pl.BlockSpec(memory_space=pltpu.VMEM)
    outs = [
        ((bands * INNER, depth), BF16),
        ((bands * SIDE, depth), BF16),
        ((bands * SIDE, depth), BF16),
        ((8, count), F32),
        ((cables, count), BF16),
    ]
    return pl.pallas_call(
        prepare_kernel,
        in_specs=[smem] + [vmem] * 3,
        out_specs=[vmem] * len(outs),
        out_shape=[jax.ShapeDtypeStruct(s, d) for s, d in outs],
        compiler_params=pltpu.CompilerParams(vmem_limit_bytes=16 << 20),
        cost_estimate=pl.CostEstimate(
            flops=2 * count * depth * bands * INNER, bytes_accessed=6 << 20, transcendentals=0
        ),
        name="prepare",
    )(band_gain, taps, index, place)


def inner_kernel(raw_ref, taps_ref, gains_ref, onehot_ref, sums_ref):
    count = raw_ref.shape[0]
    sums_ref[...] = window_sums(
        lambda part: raw_ref[part, :], taps_ref, INNER, gains_ref, None, onehot_ref, count, INNER_COLS
    )


def side_sums(is_low, edge_row, raw_ref, strip_ref, taps_ref, gains_ref, onehot_ref):
    count = raw_ref.shape[0]
    offset = pl.multiple_of(jnp.where(is_low, 0, LANES), LANES)
    beside = strip_ref[count:, :].astype(F32)

    def columns_of(part):
        return jnp.concatenate([strip_ref[part, :], raw_ref[part, pl.ds(offset, 3 * LANES)]], axis=1)

    def edges_of(start):
        rows = range(start // LANES, (start + SIDE_COLS) // LANES)
        line = jnp.concatenate([beside[a : a + 1, :] for a in rows], axis=1)
        line = line * gains_ref[edge_row : edge_row + 1, start : start + SIDE_COLS]
        return jnp.where(is_low, line, 0.0), jnp.where(is_low, 0.0, line)

    sums = window_sums(
        columns_of, taps_ref, SIDE, gains_ref, edges_of, onehot_ref, count, SIDE_COLS
    )
    depth = raw_ref.shape[1]
    sample = sample_of_row(SIDE, SIDE, depth)
    sample = sample + jnp.where(is_low, -1, depth + 1 - SIDE)
    kept = (sample >= jnp.where(is_low, 0, depth - 1 - LANES)) & (
        sample <= jnp.where(is_low, LANES, depth - 1)
    )
    col = lax.broadcasted_iota(jnp.int32, (SIDE, depth), 1)
    order = ((col == sample) & kept).astype(F32).astype(BF16)
    return jnp.dot(sums.astype(BF16), order, preferred_element_type=F32)


def near_kernel(raw_ref, strip_ref, taps_ref, gains_ref, onehot_ref, inner_ref, sums_ref):
    near = side_sums(jnp.logical_not(is_low_core()), 4, raw_ref, strip_ref, taps_ref, gains_ref, onehot_ref)
    depth = raw_ref.shape[1]
    sample = sample_of_row(INNER, INNER, depth) + LANES
    kept = (sample > LANES) & (sample < depth - LANES - 1)
    col = lax.broadcasted_iota(jnp.int32, (INNER, depth), 1)
    order = ((col == sample) & kept).astype(F32).astype(BF16)
    sums_ref[...] = near + jnp.dot(inner_ref[...].astype(BF16), order, preferred_element_type=F32)


def far_kernel(
    raw_ref, strip_ref, taps_ref, gains_ref, onehot_ref, others_ref, out_ref, scr
):
    owners, pitch, _ = out_ref.shape
    seats = others_ref.shape[0] // owners
    far = side_sums(is_low_core(), 3, raw_ref, strip_ref, taps_ref, gains_ref, onehot_ref)
    sums = others_ref[...] + far
    scr[...] = jnp.zeros_like(scr)
    tiles = sums.shape[1] // LANES
    for s in range(seats):
        for j in range(tiles):
            scr[pl.ds(tiles * s + j, owners, stride=pitch), :] = sums[
                s * owners : (s + 1) * owners, j * LANES : (j + 1) * LANES
            ]
    for o in range(owners):
        out_ref[o, :, :] = scr[o * pitch : (o + 1) * pitch, :].astype(BF16)


def window(kernel, name, out_shape, scratch, taps_at, args):
    count, depth = args[0].shape
    vmem = pl.BlockSpec(memory_space=pltpu.VMEM)
    return pl.pallas_call(
        kernel,
        in_specs=[vmem] * len(args),
        out_specs=vmem,
        out_shape=out_shape,
        scratch_shapes=scratch,
        compiler_params=pltpu.CompilerParams(vmem_limit_bytes=24 << 20),
        cost_estimate=pl.CostEstimate(
            flops=(50 if name == 'inner_window' else 1) * 2 * count * depth * 768, bytes_accessed=4<<20, transcendentals=0
        ),
        name=name,
    )(*args)


def finish_kernel(length_ref, parts_ref, out_ref):
    seats, depth = out_ref.shape
    tiles = depth // LANES
    total = jnp.sum(parts_ref[...].astype(F32), axis=0)
    for s in range(seats):
        length = length_ref[s].astype(F32)
        for j in range(tiles):
            row = tiles * s + j
            out_ref[s : s + 1, j * LANES : (j + 1) * LANES] = total[row : row + 1] / length


def finish(parts, cable_length, depth):
    return pl.pallas_call(
        finish_kernel,
        in_specs=[pl.BlockSpec(memory_space=pltpu.SMEM), pl.BlockSpec(memory_space=pltpu.VMEM)],
        out_specs=pl.BlockSpec(memory_space=pltpu.VMEM),
        out_shape=jax.ShapeDtypeStruct((cable_length.shape[0], depth), F32),
        compiler_params=pltpu.CompilerParams(vmem_limit_bytes=4 << 20),
        name="finish_sum",
    )(cable_length, parts)


def shards(raw, band_taps, band_gain, gain_index, owner_of, seat, cable_length):
    tm_count = lax.axis_size("tm")
    chan_count = lax.axis_size("chan")
    depth = raw.shape[1]
    far_pairs = [(i, i + 1) for i in range(1, tm_count - 1, 2)]
    far_pairs = far_pairs + [(j, i) for i, j in far_pairs]
    near_pairs = [(i, i ^ 1) for i in range(tm_count)]
    cab_dev = cable_length.shape[0]
    cables = cab_dev * chan_count

    blocks = raw.shape[0] // LANES
    mine = lax.axis_index("chan") * blocks
    place = lax.dynamic_slice_in_dim(seat.reshape(-1, LANES), mine, blocks, 0) * chan_count
    place = place + lax.dynamic_slice_in_dim(owner_of.reshape(-1, LANES), mine, blocks, 0)
    far_sent = pack(raw, True)
    far_strip = lax.ppermute(far_sent, "tm", far_pairs)
    near_strip = lax.ppermute(pack(raw, False, far_sent), "tm", near_pairs)
    inner_taps, far_taps, near_taps, gains, onehot = prepare(
        band_gain, band_taps, gain_index.T, place, cables, depth
    )
    inner_sums = window(
        inner_kernel, "inner_window", jax.ShapeDtypeStruct((cables, INNER), F32), [], 1,
        (raw, inner_taps, gains, onehot),
    )
    others = window(
        near_kernel, "near_window", jax.ShapeDtypeStruct((cables, depth), F32), [], 2,
        (raw, near_strip, near_taps, gains, onehot, inner_sums),
    )
    pitch = -(-(depth // LANES) * cab_dev // 8) * 8
    parts = window(
        far_kernel, "far_window", jax.ShapeDtypeStruct((chan_count, pitch, LANES), BF16),
        [pltpu.VMEM((chan_count * pitch, LANES), F32)], 2,
        (raw, far_strip, far_taps, gains, onehot, others),
    )
    parts = lax.all_to_all(parts, "chan", split_axis=0, concat_axis=0, tiled=True)
    return finish(parts, cable_length, depth)


def solution(mesh):
    return jax.shard_map(
        shards,
        mesh=mesh,
        in_specs=(P("chan", "tm"), P(), P(), P("chan", None), P(), P(), P("chan")),
        out_specs=P("chan", "tm"),
        check_vma=False,
    )
```

time: 302 us -> 41.7 us (0.14)
  the two profiles are of different devices: /device:TPU:4 before, /device:TPU:192 now
where the time goes in v1:
time: 41.7 us; the launch traced here: 41.5 us
  blocking collectives  21.5 us (52%)
  Pallas kernels  9.78 us (23%)
  starting transfers between devices  7.65 us (18%)
  local copies, waits for them, and re-layouts  1.62 us (4%)
  other arithmetic  0.72 us (2%)
    all_to_all x1, blocking collectives, shards(): lax.all_to_all(parts, 'chan', split_axis=0, concat_axis=0, tiled=True)  21.5 us
    ppermute x1, starting transfers between devices, shards(): near_strip = lax.ppermute(pack(raw, False, far_sent), 'tm', near_pairs)  5.59 us
    pallas_call x3, Pallas kernels, window(): pl.pallas_call(kernel, in_specs=[vmem] * len(args), out_specs=vmem, out_s...  5.52 us
    pallas_call x1, Pallas kernels, prepare(): pl.pallas_call(prepare_kernel, in_specs=[smem] + [vmem] * 3, out_specs=[v...  2.53 us
    ppermute x1, starting transfers between devices, shards(): far_strip = lax.ppermute(far_sent, 'tm', far_pairs)  2.05 us
    unnamed x12, local copies, waits for them, and re-layouts  1.62 us
    pallas_call x1, Pallas kernels, finish(): pl.pallas_call(finish_kernel, in_specs=[pl.BlockSpec(memory_space=pltpu.S...  1.19 us
  transfers between devices with their start and end apart: 2, of which 0 were waited for; matrix products, arithmetic and copies ran while one was open for 2% of the time, Pallas kernels for 16%

profile of v1, /device:TPU:192, one launch (start us, length us, event | category | flops | bytes accessed | tf_op | source)
XLA Modules:
  0.0 41.5 jit_solution(11457343334315565894)
XLA Ops:
  0.0 0.0 copy-start.1
  0.0 1.6 %copy-done.1 = bf16[2048,512]{1,0:T(8,128)(2,1)S(1)} copy-done((bf16[2048,512]{1,0:T(8,128)(2,1)S(1)}, bf16[2048,512]{1,0:T(8,128)(2,1)}, u32[]{:S(2)}) %copy-start.1) | copy-done | bytes 2097176
  1.6 0.3 far_strip.1.refs_0_
  1.9 0.0 copy-start.3
  1.9 0.0 copy-start.4
  1.9 0.0 copy-start.5
  1.9 2.1 %collective-permute-start = (bf16[2064,128]{1,0:T(8,128)(2,1)S(1)}, bf16[2064,128]{1,0:T(8,128)(2,1)S(1)}, u32[]{:S(2)}, u32[]{:S(2)}) collective-permute-start(bf16[2064,128]{1,0:T(8,128)(2,1)S(1)} %far_strip.1.refs_0_), channel_id=1, source_target_pairs={{32,64},{96,128},{160,192},{224,256},{288,320},{352,384},{416,448}... | collective-permute-start | bytes 1585160 | tf_op jit(solution)/shard_map/ppermute | solution.py:309
  4.0 0.3 near_strip.1
  4.2 5.6 %collective-permute-start.1 = (bf16[2064,128]{1,0:T(8,128)(2,1)S(1)}, bf16[2064,128]{1,0:T(8,128)(2,1)S(1)}, u32[]{:S(2)}, u32[]{:S(2)}) collective-permute-start(bf16[2064,128]{1,0:T(8,128)(2,1)S(1)} %near_strip.1), channel_id=1, source_target_pairs={{0,32},{32,0},{64,96},{96,64},{128,160},{160,128},{192,224},{224,1... | collective-permute-start | bytes 1585160 | tf_op jit(solution)/shard_map/ppermute | solution.py:310
  9.9 0.7 %dynamic-slice_add_fusion.place_ref = s32[16,128]{1,0:T(8,128)S(1)} fusion(s32[512,128]{1,0:T(8,128)} %bitcast.4, s32[]{:T(128)S(6)} %select_n.4, s32[512,128]{1,0:T(8,128)} %bitcast.5), kind=kLoop, calls=%fused_computation | loop fusion | flops 4096 | bytes 24580 | tf_op jit(solution)/shard_map/add | solution.py:307
  10.6 0.0 copy-done.3
  10.6 0.0 copy-done.4
  10.6 0.0 copy-done.5
  10.6 0.0 copy-start.2
  10.6 2.5 %prepare.1 = (bf16[768,512]{1,0:T(8,128)(2,1)S(1)}, bf16[432,512]{1,0:T(8,128)(2,1)S(1)}, bf16[432,512]{1,0:T(8,128)(2,1)S(1)}, f32[8,2048]{1,0:T(8,128)S(1)}, bf16[160,2048]{1,0:T(8,128)(2,1)S(1)}) custom-call(f32[16]{0:T(128)S(1)} %copy-done.5, f32[3,257]{1,0:T(4,128)S(1)} %copy-done.4, s32[3,2048]{1,0:T(4,128)S(1)} %bitcast.3, ...), custom_call_target="tpu_custom_call" | custom-call | flops 1610612736 | bytes 6291456 | tf_op jit(solution)/shard_map/prepare/pallas_call | solution.py:179
  13.1 0.0 copy-done.2
  13.2 2.3 %inner_window.1.inner_ref = f32[160,256]{1,0:T(8,128)S(1)} custom-call(bf16[2048,512]{1,0:T(8,128)(2,1)S(1)} %copy-done.2, bf16[768,512]{1,0:T(8,128)(2,1)S(1)} %get-tuple-element.14.taps_ref, f32[8,2048]{1,0:T(8,128)S(1)} %get-tuple-element.11.gains_ref, bf16[160,2048]{1,0:T(8,128)(2,1)S(1)} %get-tuple-element.12.onehot_ref), custom_call_target="tpu_custom_call" | custom-call | flops 80530636800 | bytes 4194304 | tf_op jit(solution)/shard_map/inner_window/pallas_call | solution.py:258
  15.4 0.0 collective-permute-done.1.strip_ref
  15.4 1.6 %near_window.1.others_ref = f32[160,512]{1,0:T(8,128)S(1)} custom-call(bf16[2048,512]{1,0:T(8,128)(2,1)S(1)} %copy-done.2, bf16[2064,128]{1,0:T(8,128)(2,1)S(1)} %collective-permute-done.1.strip_ref, bf16[432,512]{1,0:T(8,128)(2,1)S(1)} %get-tuple-element.13.taps_ref, f32[8,2048]{1,0:T(8,128)S(1)} %get-tuple-element.11.gains_ref, ...), custom_call_target="tpu_custom_call" | custom-call | flops 1610612736 | bytes 4194304 | tf_op jit(solution)/shard_map/near_window/pallas_call | solution.py:258
  17.1 0.0 collective-permute-done.strip_ref
  17.1 0.0 copy-start
  17.1 1.6 %far_window.1 = bf16[32,24,128]{2,1,0:T(8,128)(2,1)S(1)} custom-call(bf16[2048,512]{1,0:T(8,128)(2,1)S(1)} %copy-done.2, bf16[2064,128]{1,0:T(8,128)(2,1)S(1)} %collective-permute-done.strip_ref, bf16[432,512]{1,0:T(8,128)(2,1)S(1)} %get-tuple-element.10.taps_ref, f32[8,2048]{1,0:T(8,128)S(1)} %get-tuple-element.11.gains_ref, ...), custom_call_target="tpu_custom_call" | custom-call | flops 1610612736 | bytes 4194304 | tf_op jit(solution)/shard_map/far_window/pallas_call | solution.py:258
  18.7 21.5 %all_to_all.5.parts_ref = bf16[32,24,128]{2,1,0:T(8,128)(2,1)S(1)} all-to-all(bf16[32,24,128]{2,1,0:T(8,128)(2,1)S(1)} %far_window.1), channel_id=1, replica_groups=mesh['tm'=16,'chan'=32] {'chan'}, dimensions={0} | all-to-all | bytes 393216 | tf_op jit(solution)/shard_map/all_to_all | solution.py:328
  40.3 0.0 copy-done
  40.3 1.2 %finish_sum.1 = f32[5,512]{1,0:T(8,128)} custom-call(s32[5]{0:T(128)S(1)} %copy-done, bf16[32,24,128]{2,1,0:T(8,128)(2,1)S(1)} %all_to_all.5.parts_ref), custom_call_target="tpu_custom_call" | custom-call | tf_op jit(solution)/shard_map/finish_sum/pallas_call | solution.py:284
Async XLA Ops:
  0.0 1.6 %copy-start.1 = (bf16[2048,512]{1,0:T(8,128)(2,1)S(1)}, bf16[2048,512]{1,0:T(8,128)(2,1)}, u32[]{:S(2)}) copy-start(bf16[2048,512]{1,0:T(8,128)(2,1)} %raw_ref.9) | copy-start | bytes 6291460
  1.9 8.7 %copy-start.3 = (s32[2048,3]{0,1:T(4,128)S(1)}, s32[2048,3]{0,1:T(4,128)}, u32[]{:S(2)}) copy-start(s32[2048,3]{0,1:T(4,128)} %param.10) | copy-start | bytes 73732
  1.9 8.7 %copy-start.4 = (f32[3,257]{1,0:T(4,128)S(1)}, f32[3,257]{1,0:T(4,128)}, u32[]{:S(2)}) copy-start(f32[3,257]{1,0:T(4,128)} %taps_ref.1) | copy-start | bytes 9256
  1.9 8.7 %copy-start.5 = (f32[16]{0:T(128)S(1)}, f32[16]{0:T(128)}, u32[]{:S(2)}) copy-start(f32[16]{0:T(128)} %levels_ref.1) | copy-start | bytes 196
  1.9 15.2 %collective-permute-start = (bf16[2064,128]{1,0:T(8,128)(2,1)S(1)}, bf16[2064,128]{1,0:T(8,128)(2,1)S(1)}, u32[]{:S(2)}, u32[]{:S(2)}) collective-permute-start(bf16[2064,128]{1,0:T(8,128)(2,1)S(1)} %far_strip.1.refs_0_), channel_id=1, source_target_pairs={{32,64},{96,128},{160,192},{224,256},{288,320},{352,384},{416,448}... | collective-permute-start | bytes 1585160 | tf_op jit(solution)/shard_map/ppermute | solution.py:309
  4.2 11.2 %collective-permute-start.1 = (bf16[2064,128]{1,0:T(8,128)(2,1)S(1)}, bf16[2064,128]{1,0:T(8,128)(2,1)S(1)}, u32[]{:S(2)}, u32[]{:S(2)}) collective-permute-start(bf16[2064,128]{1,0:T(8,128)(2,1)S(1)} %near_strip.1), channel_id=1, source_target_pairs={{0,32},{32,0},{64,96},{96,64},{128,160},{160,128},{192,224},{224,1... | collective-permute-start | bytes 1585160 | tf_op jit(solution)/shard_map/ppermute | solution.py:310
  10.6 2.5 %copy-start.2 = (bf16[2048,512]{1,0:T(8,128)(2,1)S(1)}, bf16[2048,512]{1,0:T(8,128)(2,1)}, u32[]{:S(2)}) copy-start(bf16[2048,512]{1,0:T(8,128)(2,1)} %raw_ref.9) | copy-start | bytes 6291460
  17.1 23.2 %copy-start = (s32[5]{0:T(128)S(1)}, s32[5]{0:T(128)}, u32[]{:S(2)}) copy-start(s32[5]{0:T(128)} %length_ref.1) | copy-start | bytes 64

commit v2 on v1

--- a/solution.py
+++ b/solution.py
@@ -1,5 +1,3 @@
-import functools
-
 import jax
 import jax.numpy as jnp
 from jax import lax
@@ -30,30 +28,63 @@
     return lax.axis_index("tm") % 2 == 0
 
 
-def pack_kernel(is_far, raw_ref, *refs):
-    strip_ref = refs[-1]
+def fill_strip(side, raw_ref, strip_ref):
     count = raw_ref.shape[0]
-    core = lax.axis_index("tm") % 2
-    side = core if is_far else 1 - core
     strip_ref[0:count, :] = raw_ref[:, pl.ds(pl.multiple_of(side * (3 * LANES), LANES), LANES)]
     beside = raw_ref[:, pl.ds(pl.multiple_of(LANES + side * LANES, LANES), LANES)]
     strip_ref[count:, :] = beside_rows(beside, side * (LANES - 1))
 
 
-def pack(raw, is_far, *after):
-    count, depth = raw.shape
-    vmem = pl.BlockSpec(memory_space=pltpu.VMEM)
-    return pl.pallas_call(
-        functools.partial(pack_kernel, is_far),
-        in_specs=[vmem] + [pl.BlockSpec(memory_space=pl.ANY)] * len(after),
+def far_pack_kernel(raw_ref, token_ref, strip_ref):
+    del token_ref
+    fill_strip(lax.axis_index("tm") % 2, raw_ref, strip_ref)
+
+
+def near_pack_kernel(
+    raw_ref, after_ref, taps_ref, early_inner_ref, early_far_ref, early_near_ref,
+    strip_ref, inner_taps_ref, far_taps_ref, near_taps_ref,
+):
+    del after_ref
+    fill_strip(1 - lax.axis_index("tm") % 2, raw_ref, strip_ref)
+
+    @pl.when(is_low_core())
+    def _():
+        build_taps(True, taps_ref, inner_taps_ref, far_taps_ref, near_taps_ref)
+
+    @pl.when(jnp.logical_not(is_low_core()))
+    def _():
+        inner_taps_ref[...] = early_inner_ref[...]
+        far_taps_ref[...] = early_far_ref[...]
+        near_taps_ref[...] = early_near_ref[...]
+
+
+def far_pack(raw, token):
+    count = raw.shape[0]
+    vmem = pl.BlockSpec(memory_space=pltpu.VMEM)
+    return pl.pallas_call(
+        far_pack_kernel,
+        in_specs=[vmem, pl.BlockSpec(memory_space=pl.ANY)],
         out_specs=vmem,
         out_shape=jax.ShapeDtypeStruct((count + 16, LANES), BF16),
+        compiler_params=pltpu.CompilerParams(vmem_limit_bytes=8 << 20),
+        name="far_strip",
+    )(raw, token)
+
+
+def near_pack(raw, after, taps, early):
+    count, depth = raw.shape
+    vmem = pl.BlockSpec(memory_space=pltpu.VMEM)
+    return pl.pallas_call(
+        near_pack_kernel,
+        in_specs=[vmem, pl.BlockSpec(memory_space=pl.ANY)] + [vmem] * 4,
+        out_specs=[vmem] * 4,
+        out_shape=[jax.ShapeDtypeStruct((count + 16, LANES), BF16)] + tap_shapes(taps, depth),
         compiler_params=pltpu.CompilerParams(vmem_limit_bytes=8 << 20),
         cost_estimate=pl.CostEstimate(
             flops=2 * count * depth * 768, bytes_accessed=4 << 20, transcendentals=0
         ),
-        name="far_strip" if is_far else "near_strip",
-    )(raw, *after)
+        name="near_strip",
+    )(raw, after, taps, *early)
 
 
 def window_sums(columns_of, taps_ref, size, gains_ref, edges_of, onehot_ref, count, step):
@@ -85,17 +116,11 @@
     return jnp.bitwise_and(row, 7) * (size // 8) + jnp.right_shift(row, 3)
 
 
-def prepare_kernel(
-    levels_ref, taps_ref, index_ref, place_ref,
-    inner_taps_ref, far_taps_ref, near_taps_ref, gains_ref, onehot_ref,
-):
-    is_low = is_low_core()
+def build_taps(is_low, taps_ref, inner_taps_ref, far_taps_ref, near_taps_ref):
     tm_pos = lax.axis_index("tm")
     inside = jnp.logical_and(tm_pos > 0, tm_pos < lax.axis_size("tm") - 1).astype(F32)
-    count = index_ref.shape[1]
     depth = inner_taps_ref.shape[1]
     bands, width = taps_ref.shape
-    blocks = count // LANES
     wide = depth + LANES
 
     reach = 3 * LANES
@@ -128,24 +153,51 @@
             at = b * INNER + 8 * j
             inner_taps_ref[at : at + 16, :] = jnp.concatenate(rows[j : j + 2], axis=0).astype(BF16)
         low, high = rows_of(b, SIDE, (-1, 2 * LANES + 1 - SIDE))
-        low[0] = jnp.where(sub == 0, low[0] * jnp.where(is_low, inside, 1.0), low[0])
-        high[-1] = jnp.where(sub == 7, high[-1] * jnp.where(is_low, 1.0, inside), high[-1])
+        if is_low:
+            low[0] = jnp.where(sub == 0, low[0] * inside, low[0])
+        else:
+            high[-1] = jnp.where(sub == 7, high[-1] * inside, high[-1])
         for j in range(0, SIDE // 8, 2):
             at = slice(b * SIDE + 8 * j, b * SIDE + 8 * j + 16)
             low_rows = jnp.concatenate(low[j : j + 2], axis=0).astype(BF16)
             high_rows = jnp.concatenate(high[j : j + 2], axis=0).astype(BF16)
             high_rows = jnp.concatenate([high_rows[:, 3 * LANES :], high_rows[:, : 3 * LANES]], axis=1)
 
-            @pl.when(is_low)
-            def _():
-                far_taps_ref[at, :] = low_rows
-                near_taps_ref[at, :] = high_rows
-
-            @pl.when(jnp.logical_not(is_low))
-            def _():
-                far_taps_ref[at, :] = high_rows
-                near_taps_ref[at, :] = low_rows
-
+            far_taps_ref[at, :], near_taps_ref[at, :] = (
+                (low_rows, high_rows) if is_low else (high_rows, low_rows)
+            )
+
+
+def early_taps_kernel(taps_ref, inner_taps_ref, far_taps_ref, near_taps_ref, token_ref):
+    token_ref[...] = jnp.zeros_like(token_ref)
+
+    @pl.when(jnp.logical_not(is_low_core()))
+    def _():
+        build_taps(False, taps_ref, inner_taps_ref, far_taps_ref, near_taps_ref)
+
+
+def tap_shapes(taps, depth):
+    rows = (INNER, SIDE, SIDE)
+    return [jax.ShapeDtypeStruct((taps.shape[0] * r, depth), BF16) for r in rows]
+
+
+def early_taps(taps, depth):
+    vmem = pl.BlockSpec(memory_space=pltpu.VMEM)
+    return pl.pallas_call(
+        early_taps_kernel,
+        in_specs=[vmem],
+        out_specs=[vmem] * 4,
+        out_shape=tap_shapes(taps, depth) + [jax.ShapeDtypeStruct((8, LANES), F32)],
+        compiler_params=pltpu.CompilerParams(vmem_limit_bytes=8 << 20),
+        cost_estimate=pl.CostEstimate(flops=3 << 30, bytes_accessed=6 << 20, transcendentals=0),
+        name="early_taps",
+    )(taps)
+
+
+def channels_kernel(levels_ref, taps_ref, index_ref, owner_ref, seat_ref, gains_ref, onehot_ref):
+    is_low = is_low_core()
+    bands, width = taps_ref.shape
+    blocks = index_ref.shape[1] // LANES
     index = index_ref[...]
     gains = jnp.zeros(index.shape, F32)
     for level in range(levels_ref.shape[0]):
@@ -158,35 +210,28 @@
     gains_ref[0:bands, :] = gains
     gains_ref[3:4, :] = jnp.where(is_low, low_edge, high_edge)
     gains_ref[4:5, :] = jnp.where(is_low, high_edge, low_edge)
-    place = place_ref[...]
+    mine = pl.ds(pl.multiple_of(lax.axis_index("chan") * blocks, blocks), blocks)
+    place = seat_ref[mine, :] * lax.axis_size("chan") + owner_ref[mine, :]
     cable = lax.broadcasted_iota(jnp.int32, (onehot_ref.shape[0], LANES), 0)
     for a in range(blocks):
         onehot_ref[:, a * LANES : (a + 1) * LANES] = (cable == place[a : a + 1, :]).astype(F32).astype(BF16)
 
 
-def prepare(band_gain, taps, index, place, cables, depth):
+def channel_tables(band_gain, taps, index, owner, seat, cables):
     count = index.shape[1]
-    bands = taps.shape[0]
-    smem = pl.BlockSpec(memory_space=pltpu.SMEM)
-    vmem = pl.BlockSpec(memory_space=pltpu.VMEM)
-    outs = [
-        ((bands * INNER, depth), BF16),
-        ((bands * SIDE, depth), BF16),
-        ((bands * SIDE, depth), BF16),
-        ((8, count), F32),
-        ((cables, count), BF16),
-    ]
-    return pl.pallas_call(
-        prepare_kernel,
-        in_specs=[smem] + [vmem] * 3,
-        out_specs=[vmem] * len(outs),
-        out_shape=[jax.ShapeDtypeStruct(s, d) for s, d in outs],
-        compiler_params=pltpu.CompilerParams(vmem_limit_bytes=16 << 20),
-        cost_estimate=pl.CostEstimate(
-            flops=2 * count * depth * bands * INNER, bytes_accessed=6 << 20, transcendentals=0
-        ),
-        name="prepare",
-    )(band_gain, taps, index, place)
+    vmem = pl.BlockSpec(memory_space=pltpu.VMEM)
+    return pl.pallas_call(
+        channels_kernel,
+        in_specs=[pl.BlockSpec(memory_space=pltpu.SMEM)] + [vmem] * 4,
+        out_specs=[vmem] * 2,
+        out_shape=[
+            jax.ShapeDtypeStruct((8, count), F32),
+            jax.ShapeDtypeStruct((cables, count), BF16),
+        ],
+        compiler_params=pltpu.CompilerParams(vmem_limit_bytes=8 << 20),
+        cost_estimate=pl.CostEstimate(flops=1 << 30, bytes_accessed=1 << 20, transcendentals=0),
+        name="channel_tables",
+    )(band_gain, taps, index, owner, seat)
 
 
 def inner_kernel(raw_ref, taps_ref, gains_ref, onehot_ref, sums_ref):
@@ -301,15 +346,13 @@
     cab_dev = cable_length.shape[0]
     cables = cab_dev * chan_count
 
-    blocks = raw.shape[0] // LANES
-    mine = lax.axis_index("chan") * blocks
-    place = lax.dynamic_slice_in_dim(seat.reshape(-1, LANES), mine, blocks, 0) * chan_count
-    place = place + lax.dynamic_slice_in_dim(owner_of.reshape(-1, LANES), mine, blocks, 0)
-    far_sent = pack(raw, True)
+    *early, token = early_taps(band_taps, depth)
+    far_sent = far_pack(raw, token)
     far_strip = lax.ppermute(far_sent, "tm", far_pairs)
-    near_strip = lax.ppermute(pack(raw, False, far_sent), "tm", near_pairs)
-    inner_taps, far_taps, near_taps, gains, onehot = prepare(
-        band_gain, band_taps, gain_index.T, place, cables, depth
+    near_sent, inner_taps, far_taps, near_taps = near_pack(raw, far_sent, band_taps, early)
+    near_strip = lax.ppermute(near_sent, "tm", near_pairs)
+    gains, onehot = channel_tables(
+        band_gain, band_taps, gain_index.T, owner_of.reshape(-1, LANES), seat.reshape(-1, LANES), cables
     )
     inner_sums = window(
         inner_kernel, "inner_window", jax.ShapeDtypeStruct((cables, INNER), F32), [], 1,

time: 41.7 us -> 39.4 us (0.945)
  starting transfers between devices: 7.65 us -> 6.38 us
  other arithmetic: 0.72 us -> 0 us
    ppermute x1, starting transfers between devices: 5.59 us -> 4.46 us  [shards(): near_strip = lax.ppermute(near_sent, 'tm', near_pairs)]
    add x1 -> x0, other arithmetic: 0.72 us -> none  [shards(): place + lax.dynamic_slice_in_dim(owner_of.reshape(-1, LANES), mine, block...]
    pallas_call x3 -> x4, Pallas kernels: 3.07 us -> 2.66 us  [the longest x1 1.51 us: near_pack(): pl.pallas_call(near_pack_kernel, in_specs=[vmem, pl.BlockSpec(memory_spac...]
    unnamed x12 -> x14, local copies, waits for them, and re-layouts: 1.62 us -> 1.63 us
  transfers between devices with their start and end apart: 2 -> 2, of which waited for: 0 -> 0; matrix products, arithmetic and copies ran while one was open for 2% -> 0% of each run, Pallas kernels for 16% -> 16%
where the time goes in v2:
time: 39.4 us; the launch traced here: 39.2 us
  blocking collectives  21.5 us (55%)
  Pallas kernels  9.49 us (24%)
  starting transfers between devices  6.38 us (16%)
  local copies, waits for them, and re-layouts  1.63 us (4%)
    all_to_all x1, blocking collectives, shards(): lax.all_to_all(parts, 'chan', split_axis=0, concat_axis=0, tiled=True)  21.5 us
    pallas_call x3, Pallas kernels, window(): pl.pallas_call(kernel, in_specs=[vmem] * len(args), out_specs=vmem, out_s...  5.64 us
    ppermute x1, starting transfers between devices, shards(): near_strip = lax.ppermute(near_sent, 'tm', near_pairs)  4.46 us
    ppermute x1, starting transfers between devices, shards(): far_strip = lax.ppermute(far_sent, 'tm', far_pairs)  1.92 us
    unnamed x14, local copies, waits for them, and re-layouts  1.63 us
    pallas_call x1, Pallas kernels, near_pack(): pl.pallas_call(near_pack_kernel, in_specs=[vmem, pl.BlockSpec(memory_spac...  1.51 us
    pallas_call x1, Pallas kernels, finish(): pl.pallas_call(finish_kernel, in_specs=[pl.BlockSpec(memory_space=pltpu.S...  1.19 us
    pallas_call x1, Pallas kernels, channel_tables(): pl.pallas_call(channels_kernel, in_specs=[pl.BlockSpec(memory_space=pltpu...  0.88 us
  transfers between devices with their start and end apart: 2, of which 0 were waited for; matrix products, arithmetic and copies ran while one was open for 0% of the time, Pallas kernels for 16%

profile of v2, /device:TPU:192, one launch (start us, length us, event | category | flops | bytes accessed | tf_op | source)
XLA Modules:
  0.0 39.2 jit_solution(69409466209084947)
XLA Ops:
  0.0 0.0 copy-start
  0.0 0.0 copy-start.5
  0.0 0.8 %copy-done.5 = f32[3,257]{1,0:T(4,128)S(1)} copy-done((f32[3,257]{1,0:T(4,128)S(1)}, f32[3,257]{1,0:T(4,128)}, u32[]{:S(2)}) %copy-start.5) | copy-done | bytes 3108
  0.8 0.8 %copy-done = bf16[2048,512]{1,0:T(8,128)(2,1)S(1)} copy-done((bf16[2048,512]{1,0:T(8,128)(2,1)S(1)}, bf16[2048,512]{1,0:T(8,128)(2,1)}, u32[]{:S(2)}) %copy-start) | copy-done | bytes 2097176
  1.6 0.3 far_strip.1.after_ref
  1.9 1.9 %collective-permute-start = (bf16[2064,128]{1,0:T(8,128)(2,1)S(1)}, bf16[2064,128]{1,0:T(8,128)(2,1)S(1)}, u32[]{:S(2)}, u32[]{:S(2)}) collective-permute-start(bf16[2064,128]{1,0:T(8,128)(2,1)S(1)} %far_strip.1.after_ref), channel_id=1, source_target_pairs={{32,64},{96,128},{160,192},{224,256},{288,320},{352,384},{416,448}... | collective-permute-start | bytes 1585160 | tf_op jit(solution)/shard_map/ppermute | solution.py:351
  3.8 0.0 copy-start.2
  3.8 0.0 copy-start.3
  3.8 0.0 copy-start.4
  3.8 0.0 copy-start.6
  3.9 1.5 %near_strip.1 = (bf16[2064,128]{1,0:T(8,128)(2,1)S(1)}, bf16[768,512]{1,0:T(8,128)(2,1)S(1)}, bf16[432,512]{1,0:T(8,128)(2,1)S(1)}, bf16[432,512]{1,0:T(8,128)(2,1)S(1)}) custom-call(bf16[2048,512]{1,0:T(8,128)(2,1)S(1)} %copy-done, bf16[2064,128]{1,0:T(8,128)(2,1)S(1)} %far_strip.1.after_ref, f32[3,257]{1,0:T(4,128)S(1)} %copy-done.5, ...), custom_call_target="tpu_custom_call" | custom-call | flops 1610612736 | bytes 4194304 | tf_op jit(solution)/shard_map/near_strip/pallas_call | solution.py:77
  5.4 4.5 %collective-permute-start.1 = (bf16[2064,128]{1,0:T(8,128)(2,1)S(1)}, bf16[2064,128]{1,0:T(8,128)(2,1)S(1)}, u32[]{:S(2)}, u32[]{:S(2)}) collective-permute-start(bf16[2064,128]{1,0:T(8,128)(2,1)S(1)} %get-tuple-element.22), channel_id=1, source_target_pairs={{0,32},{32,0},{64,96},{96,64},{128,160},{160,128},{192,224},{224,1... | collective-permute-start | bytes 1585160 | tf_op jit(solution)/shard_map/ppermute | solution.py:353
  9.8 0.0 copy-done.2
  9.9 0.0 copy-done.3
  9.9 0.0 copy-done.4
  9.9 0.0 copy-done.6
  9.9 0.9 %channel_tables.1 = (f32[8,2048]{1,0:T(8,128)S(1)}, bf16[160,2048]{1,0:T(8,128)(2,1)S(1)}) custom-call(f32[16]{0:T(128)S(1)} %copy-done.6, f32[3,257]{1,0:T(4,128)S(1)} %copy-done.5, s32[3,2048]{1,0:T(4,128)S(1)} %bitcast.5, s32[512,128]{1,0:T(8,128)S(1)} %bitcast.3, s32[512,128]{1,0:T(8,128)S(1)} %bitcast.4), custom_call_target="tpu_custom_call" | custom-call | flops 1073741824 | bytes 1048576 | tf_op jit(solution)/shard_map/channel_tables/pallas_call | solution.py:223
  10.8 2.3 %inner_window.1.inner_ref = f32[160,256]{1,0:T(8,128)S(1)} custom-call(bf16[2048,512]{1,0:T(8,128)(2,1)S(1)} %copy-done, bf16[768,512]{1,0:T(8,128)(2,1)S(1)} %get-tuple-element.24.taps_ref, f32[8,2048]{1,0:T(8,128)S(1)} %get-tuple-element.20.gains_ref, bf16[160,2048]{1,0:T(8,128)(2,1)S(1)} %get-tuple-element.21.onehot_ref), custom_call_target="tpu_custom_call" | custom-call | flops 80530636800 | bytes 4194304 | tf_op jit(solution)/shard_map/inner_window/pallas_call | solution.py:303
  13.1 0.0 collective-permute-done.1.strip_ref
  13.1 1.6 %near_window.1.others_ref = f32[160,512]{1,0:T(8,128)S(1)} custom-call(bf16[2048,512]{1,0:T(8,128)(2,1)S(1)} %copy-done, bf16[2064,128]{1,0:T(8,128)(2,1)S(1)} %collective-permute-done.1.strip_ref, bf16[432,512]{1,0:T(8,128)(2,1)S(1)} %get-tuple-element.23.taps_ref, f32[8,2048]{1,0:T(8,128)S(1)} %get-tuple-element.20.gains_ref, ...), custom_call_target="tpu_custom_call" | custom-call | flops 1610612736 | bytes 4194304 | tf_op jit(solution)/shard_map/near_window/pallas_call | solution.py:303
  14.8 0.0 collective-permute-done.strip_ref
  14.8 0.0 copy-start.1
  14.8 1.7 %far_window.1 = bf16[32,24,128]{2,1,0:T(8,128)(2,1)S(1)} custom-call(bf16[2048,512]{1,0:T(8,128)(2,1)S(1)} %copy-done, bf16[2064,128]{1,0:T(8,128)(2,1)S(1)} %collective-permute-done.strip_ref, bf16[432,512]{1,0:T(8,128)(2,1)S(1)} %get-tuple-element.19.taps_ref, f32[8,2048]{1,0:T(8,128)S(1)} %get-tuple-element.20.gains_ref, ...), custom_call_target="tpu_custom_call" | custom-call | flops 1610612736 | bytes 4194304 | tf_op jit(solution)/shard_map/far_window/pallas_call | solution.py:303
  16.5 21.5 %all_to_all.5.parts_ref = bf16[32,24,128]{2,1,0:T(8,128)(2,1)S(1)} all-to-all(bf16[32,24,128]{2,1,0:T(8,128)(2,1)S(1)} %far_window.1), channel_id=1, replica_groups=mesh['tm'=16,'chan'=32] {'chan'}, dimensions={0} | all-to-all | bytes 393216 | tf_op jit(solution)/shard_map/all_to_all | solution.py:371
  38.0 0.0 copy-done.1
  38.0 1.2 %finish_sum.1 = f32[5,512]{1,0:T(8,128)} custom-call(s32[5]{0:T(128)S(1)} %copy-done.1, bf16[32,24,128]{2,1,0:T(8,128)(2,1)S(1)} %all_to_all.5.parts_ref), custom_call_target="tpu_custom_call" | custom-call | tf_op jit(solution)/shard_map/finish_sum/pallas_call | solution.py:329
  (1 shorter events, 0.0 us)
Async XLA Ops:
  0.0 1.6 %copy-start = (bf16[2048,512]{1,0:T(8,128)(2,1)S(1)}, bf16[2048,512]{1,0:T(8,128)(2,1)}, u32[]{:S(2)}) copy-start(bf16[2048,512]{1,0:T(8,128)(2,1)} %raw_ref.9) | copy-start | bytes 6291460
  0.0 0.8 %copy-start.5 = (f32[3,257]{1,0:T(4,128)S(1)}, f32[3,257]{1,0:T(4,128)}, u32[]{:S(2)}) copy-start(f32[3,257]{1,0:T(4,128)} %taps_ref.5) | copy-start | bytes 9256
  1.9 12.9 %collective-permute-start = (bf16[2064,128]{1,0:T(8,128)(2,1)S(1)}, bf16[2064,128]{1,0:T(8,128)(2,1)S(1)}, u32[]{:S(2)}, u32[]{:S(2)}) collective-permute-start(bf16[2064,128]{1,0:T(8,128)(2,1)S(1)} %far_strip.1.after_ref), channel_id=1, source_target_pairs={{32,64},{96,128},{160,192},{224,256},{288,320},{352,384},{416,448}... | collective-permute-start | bytes 1585160 | tf_op jit(solution)/shard_map/ppermute | solution.py:351
  3.8 6.0 %copy-start.2 = (s32[65536,1]{0,1:T(1,128)S(1)}, s32[65536,1]{0,1:T(1,128)}, u32[]{:S(2)}) copy-start(s32[65536,1]{0,1:T(1,128)} %param.11) | copy-start | bytes 786436
  3.8 6.0 %copy-start.3 = (s32[65536]{0:T(1024)S(1)}, s32[65536]{0:T(1024)}, u32[]{:S(2)}) copy-start(s32[65536]{0:T(1024)} %param.12) | copy-start | bytes 786436
  3.8 6.0 %copy-start.4 = (s32[2048,3]{0,1:T(4,128)S(1)}, s32[2048,3]{0,1:T(4,128)}, u32[]{:S(2)}) copy-start(s32[2048,3]{0,1:T(4,128)} %param.10) | copy-start | bytes 73732
  3.8 6.0 %copy-start.6 = (f32[16]{0:T(128)S(1)}, f32[16]{0:T(128)}, u32[]{:S(2)}) copy-start(f32[16]{0:T(128)} %levels_ref.1) | copy-start | bytes 196
  5.4 7.7 %collective-permute-start.1 = (bf16[2064,128]{1,0:T(8,128)(2,1)S(1)}, bf16[2064,128]{1,0:T(8,128)(2,1)S(1)}, u32[]{:S(2)}, u32[]{:S(2)}) collective-permute-start(bf16[2064,128]{1,0:T(8,128)(2,1)S(1)} %get-tuple-element.22), channel_id=1, source_target_pairs={{0,32},{32,0},{64,96},{96,64},{128,160},{160,128},{192,224},{224,1... | collective-permute-start | bytes 1585160 | tf_op jit(solution)/shard_map/ppermute | solution.py:353
  14.8 23.2 %copy-start.1 = (s32[5]{0:T(128)S(1)}, s32[5]{0:T(128)}, u32[]{:S(2)}) copy-start(s32[5]{0:T(128)} %length_ref.1) | copy-start | bytes 64

commit v3 on v2

--- a/solution.py
+++ b/solution.py
@@ -35,9 +35,30 @@
     strip_ref[count:, :] = beside_rows(beside, side * (LANES - 1))
 
 
-def far_pack_kernel(raw_ref, token_ref, strip_ref):
-    del token_ref
-    fill_strip(lax.axis_index("tm") % 2, raw_ref, strip_ref)
+def first_kernel(
+    raw_ref, taps_ref, strip_ref, inner_taps_ref, far_taps_ref, near_taps_ref, beside, taps, sems
+):
+    side = lax.axis_index("tm") % 2
+    count = raw_ref.shape[0]
+    at = pl.multiple_of(side * (3 * LANES), LANES)
+    by = pl.multiple_of(LANES + side * LANES, LANES)
+    jobs = [
+        pltpu.make_async_copy(raw_ref.at[:, pl.ds(by, LANES)], beside, sems.at[0]),
+        pltpu.make_async_copy(raw_ref.at[:, pl.ds(at, LANES)], strip_ref.at[0:count], sems.at[1]),
+    ]
+    for job in jobs:
+        job.start()
+
+    @pl.when(side == 1)
+    def _():
+        job = pltpu.make_async_copy(taps_ref, taps, sems.at[2])
+        job.start()
+        job.wait()
+        build_taps(False, taps, inner_taps_ref, far_taps_ref, near_taps_ref)
+
+    jobs[0].wait()
+    strip_ref[count:, :] = beside_rows(beside[...], side * (LANES - 1))
+    jobs[1].wait()
 
 
 def near_pack_kernel(
@@ -58,17 +79,22 @@
         near_taps_ref[...] = early_near_ref[...]
 
 
-def far_pack(raw, token):
-    count = raw.shape[0]
-    vmem = pl.BlockSpec(memory_space=pltpu.VMEM)
-    return pl.pallas_call(
-        far_pack_kernel,
-        in_specs=[vmem, pl.BlockSpec(memory_space=pl.ANY)],
-        out_specs=vmem,
-        out_shape=jax.ShapeDtypeStruct((count + 16, LANES), BF16),
-        compiler_params=pltpu.CompilerParams(vmem_limit_bytes=8 << 20),
+def first(raw, taps):
+    count, depth = raw.shape
+    outs = [jax.ShapeDtypeStruct((count + 16, LANES), BF16)] + tap_shapes(taps, depth)
+    return pl.pallas_call(
+        first_kernel,
+        in_specs=[pl.BlockSpec(memory_space=pltpu.HBM)] * 2,
+        out_specs=[pl.BlockSpec(memory_space=pltpu.VMEM)] * len(outs),
+        out_shape=outs,
+        scratch_shapes=[
+            pltpu.VMEM((count, LANES), BF16),
+            pltpu.VMEM(taps.shape, F32),
+            pltpu.SemaphoreType.DMA((3,)),
+        ],
+        compiler_params=pltpu.CompilerParams(vmem_limit_bytes=16 << 20),
         name="far_strip",
-    )(raw, token)
+    )(*[pltpu.with_memory_space_constraint(a, pltpu.HBM) for a in (raw, taps)])
 
 
 def near_pack(raw, after, taps, early):
@@ -168,33 +194,14 @@
             )
 
 
-def early_taps_kernel(taps_ref, inner_taps_ref, far_taps_ref, near_taps_ref, token_ref):
-    token_ref[...] = jnp.zeros_like(token_ref)
-
-    @pl.when(jnp.logical_not(is_low_core()))
-    def _():
-        build_taps(False, taps_ref, inner_taps_ref, far_taps_ref, near_taps_ref)
-
-
 def tap_shapes(taps, depth):
     rows = (INNER, SIDE, SIDE)
     return [jax.ShapeDtypeStruct((taps.shape[0] * r, depth), BF16) for r in rows]
 
 
-def early_taps(taps, depth):
-    vmem = pl.BlockSpec(memory_space=pltpu.VMEM)
-    return pl.pallas_call(
-        early_taps_kernel,
-        in_specs=[vmem],
-        out_specs=[vmem] * 4,
-        out_shape=tap_shapes(taps, depth) + [jax.ShapeDtypeStruct((8, LANES), F32)],
-        compiler_params=pltpu.CompilerParams(vmem_limit_bytes=8 << 20),
-        cost_estimate=pl.CostEstimate(flops=3 << 30, bytes_accessed=6 << 20, transcendentals=0),
-        name="early_taps",
-    )(taps)
-
-
-def channels_kernel(levels_ref, taps_ref, index_ref, owner_ref, seat_ref, gains_ref, onehot_ref):
+def channels_kernel(
+    levels_ref, length_ref, taps_ref, index_ref, owner_ref, seat_ref, gains_ref, onehot_ref, divisor_ref
+):
     is_low = is_low_core()
     bands, width = taps_ref.shape
     blocks = index_ref.shape[1] // LANES
@@ -215,23 +222,28 @@
     cable = lax.broadcasted_iota(jnp.int32, (onehot_ref.shape[0], LANES), 0)
     for a in range(blocks):
         onehot_ref[:, a * LANES : (a + 1) * LANES] = (cable == place[a : a + 1, :]).astype(F32).astype(BF16)
-
-
-def channel_tables(band_gain, taps, index, owner, seat, cables):
+    tiles = divisor_ref.shape[0] // length_ref.shape[0]
+    divisor_ref[...] = jnp.ones_like(divisor_ref)
+    for k in range(length_ref.shape[0]):
+        divisor_ref[k * tiles : (k + 1) * tiles, :] = jnp.full((tiles, LANES), length_ref[k].astype(F32))
+
+
+def channel_tables(band_gain, cable_length, taps, index, owner, seat, cables, pitch):
     count = index.shape[1]
     vmem = pl.BlockSpec(memory_space=pltpu.VMEM)
     return pl.pallas_call(
         channels_kernel,
-        in_specs=[pl.BlockSpec(memory_space=pltpu.SMEM)] + [vmem] * 4,
-        out_specs=[vmem] * 2,
+        in_specs=[pl.BlockSpec(memory_space=pltpu.SMEM)] * 2 + [vmem] * 4,
+        out_specs=[vmem] * 3,
         out_shape=[
             jax.ShapeDtypeStruct((8, count), F32),
             jax.ShapeDtypeStruct((cables, count), BF16),
+            jax.ShapeDtypeStruct((pitch, LANES), F32),
         ],
         compiler_params=pltpu.CompilerParams(vmem_limit_bytes=8 << 20),
         cost_estimate=pl.CostEstimate(flops=1 << 30, bytes_accessed=1 << 20, transcendentals=0),
         name="channel_tables",
-    )(band_gain, taps, index, owner, seat)
+    )(band_gain, cable_length, taps, index, owner, seat)
 
 
 def inner_kernel(raw_ref, taps_ref, gains_ref, onehot_ref, sums_ref):
@@ -286,8 +298,9 @@
     seats = others_ref.shape[0] // owners
     far = side_sums(is_low_core(), 3, raw_ref, strip_ref, taps_ref, gains_ref, onehot_ref)
     sums = others_ref[...] + far
-    scr[...] = jnp.zeros_like(scr)
     tiles = sums.shape[1] // LANES
+    for spare in range(tiles * seats, pitch):
+        scr[pl.ds(spare, owners, stride=pitch), :] = jnp.zeros((owners, LANES), F32)
     for s in range(seats):
         for j in range(tiles):
             scr[pl.ds(tiles * s + j, owners, stride=pitch), :] = sums[
@@ -314,26 +327,26 @@
     )(*args)
 
 
-def finish_kernel(length_ref, parts_ref, out_ref):
+def finish_kernel(divisor_ref, parts_ref, out_ref):
     seats, depth = out_ref.shape
     tiles = depth // LANES
-    total = jnp.sum(parts_ref[...].astype(F32), axis=0)
+    total = jnp.sum(parts_ref[...].astype(F32), axis=0) / divisor_ref[...]
     for s in range(seats):
-        length = length_ref[s].astype(F32)
         for j in range(tiles):
             row = tiles * s + j
-            out_ref[s : s + 1, j * LANES : (j + 1) * LANES] = total[row : row + 1] / length
-
-
-def finish(parts, cable_length, depth):
+            out_ref[s : s + 1, j * LANES : (j + 1) * LANES] = total[row : row + 1]
+
+
+def finish(parts, divisor, seats, depth):
+    vmem = pl.BlockSpec(memory_space=pltpu.VMEM)
     return pl.pallas_call(
         finish_kernel,
-        in_specs=[pl.BlockSpec(memory_space=pltpu.SMEM), pl.BlockSpec(memory_space=pltpu.VMEM)],
-        out_specs=pl.BlockSpec(memory_space=pltpu.VMEM),
-        out_shape=jax.ShapeDtypeStruct((cable_length.shape[0], depth), F32),
+        in_specs=[vmem, vmem],
+        out_specs=vmem,
+        out_shape=jax.ShapeDtypeStruct((seats, depth), F32),
         compiler_params=pltpu.CompilerParams(vmem_limit_bytes=4 << 20),
         name="finish_sum",
-    )(cable_length, parts)
+    )(divisor, parts)
 
 
 def shards(raw, band_taps, band_gain, gain_index, owner_of, seat, cable_length):
@@ -346,13 +359,14 @@
     cab_dev = cable_length.shape[0]
     cables = cab_dev * chan_count
 
-    *early, token = early_taps(band_taps, depth)
-    far_sent = far_pack(raw, token)
+    far_sent, *early = first(raw, band_taps)
     far_strip = lax.ppermute(far_sent, "tm", far_pairs)
     near_sent, inner_taps, far_taps, near_taps = near_pack(raw, far_sent, band_taps, early)
     near_strip = lax.ppermute(near_sent, "tm", near_pairs)
-    gains, onehot = channel_tables(
-        band_gain, band_taps, gain_index.T, owner_of.reshape(-1, LANES), seat.reshape(-1, LANES), cables
+    pitch = -(-(depth // LANES) * cab_dev // 8) * 8
+    gains, onehot, divisor = channel_tables(
+        band_gain, cable_length, band_taps, gain_index.T,
+        owner_of.reshape(-1, LANES), seat.reshape(-1, LANES), cables, pitch,
     )
     inner_sums = window(
         inner_kernel, "inner_window", jax.ShapeDtypeStruct((cables, INNER), F32), [], 1,
@@ -362,14 +376,13 @@
         near_kernel, "near_window", jax.ShapeDtypeStruct((cables, depth), F32), [], 2,
         (raw, near_strip, near_taps, gains, onehot, inner_sums),
     )
-    pitch = -(-(depth // LANES) * cab_dev // 8) * 8
     parts = window(
         far_kernel, "far_window", jax.ShapeDtypeStruct((chan_count, pitch, LANES), BF16),
         [pltpu.VMEM((chan_count * pitch, LANES), F32)], 2,
         (raw, far_strip, far_taps, gains, onehot, others),
     )
     parts = lax.all_to_all(parts, "chan", split_axis=0, concat_axis=0, tiled=True)
-    return finish(parts, cable_length, depth)
+    return finish(parts, divisor, cab_dev, depth)
 
 
 def solution(mesh):

time: 39.4 us -> 38.5 us (0.977)
  local copies, waits for them, and re-layouts: 1.63 us -> 0.04 us
  Pallas kernels: 9.49 us -> 10.2 us
    unnamed x14, local copies, waits for them, and re-layouts: 1.63 us -> 0.04 us
    pallas_call x3 -> x2, Pallas kernels: 1.46 us -> 2.13 us  [the longest x1 1.47 us: first(): pl.pallas_call(first_kernel, in_specs=[pl.BlockSpec(memory_space=pltpu.HB...]
  transfers between devices with their start and end apart: 2 -> 2, of which waited for: 0 -> 0; matrix products, arithmetic and copies ran while one was open for 0% -> 0% of each run, Pallas kernels for 16% -> 17%
where the time goes in v3:
time: 38.5 us; the launch traced here: 38.3 us
  blocking collectives  21.5 us (56%)
  Pallas kernels  10.2 us (26%)
  starting transfers between devices  6.38 us (17%)
    all_to_all x1, blocking collectives, shards(): lax.all_to_all(parts, 'chan', split_axis=0, concat_axis=0, tiled=True)  21.5 us
    pallas_call x3, Pallas kernels, window(): pl.pallas_call(kernel, in_specs=[vmem] * len(args), out_specs=vmem, out_s...  5.65 us
    ppermute x1, starting transfers between devices, shards(): near_strip = lax.ppermute(near_sent, 'tm', near_pairs)  4.14 us
    ppermute x1, starting transfers between devices, shards(): far_strip = lax.ppermute(far_sent, 'tm', far_pairs)  2.24 us
    pallas_call x1, Pallas kernels, near_pack(): pl.pallas_call(near_pack_kernel, in_specs=[vmem, pl.BlockSpec(memory_spac...  1.51 us
    pallas_call x1, Pallas kernels, first(): pl.pallas_call(first_kernel, in_specs=[pl.BlockSpec(memory_space=pltpu.HB...  1.47 us
    pallas_call x1, Pallas kernels, channel_tables(): pl.pallas_call(channels_kernel, in_specs=[pl.BlockSpec(memory_space=pltpu...  0.88 us
  transfers between devices with their start and end apart: 2, of which 0 were waited for; matrix products, arithmetic and copies ran while one was open for 0% of the time, Pallas kernels for 17%

profile of v3, /device:TPU:192, one launch (start us, length us, event | category | flops | bytes accessed | tf_op | source)
XLA Modules:
  0.0 38.3 jit_solution(18189400550919550759)
XLA Ops:
  0.0 0.0 copy-start
  0.0 0.0 copy-start.1
  0.0 1.5 %far_strip.1 = (bf16[2064,128]{1,0:T(8,128)(2,1)S(1)}, bf16[768,512]{1,0:T(8,128)(2,1)S(1)}, bf16[432,512]{1,0:T(8,128)(2,1)S(1)}, bf16[432,512]{1,0:T(8,128)(2,1)S(1)}) custom-call(bf16[2048,512]{1,0:T(8,128)(2,1)} %raw_ref.9, f32[3,257]{1,0:T(4,128)} %taps_ref.5), custom_call_target="tpu_custom_call" | custom-call | tf_op jit(solution)/shard_map/far_strip/pallas_call | solution.py:85
  1.5 2.2 %collective-permute-start = (bf16[2064,128]{1,0:T(8,128)(2,1)S(1)}, bf16[2064,128]{1,0:T(8,128)(2,1)S(1)}, u32[]{:S(2)}, u32[]{:S(2)}) collective-permute-start(bf16[2064,128]{1,0:T(8,128)(2,1)S(1)} %get-tuple-element.17.after_ref), channel_id=1, source_target_pairs={{32,64},{96,128},{160,192},{224,256},{288,320},{352,384},{416,448}... | collective-permute-start | bytes 1585160 | tf_op jit(solution)/shard_map/ppermute | solution.py:363
  3.7 0.0 copy-done
  3.7 0.0 copy-done.1
  3.8 0.0 copy-start.2
  3.8 0.0 copy-start.3
  3.8 0.0 copy-start.4
  3.8 0.0 copy-start.5
  3.8 0.0 copy-start.6
  3.8 1.5 %near_strip.1 = (bf16[2064,128]{1,0:T(8,128)(2,1)S(1)}, bf16[768,512]{1,0:T(8,128)(2,1)S(1)}, bf16[432,512]{1,0:T(8,128)(2,1)S(1)}, bf16[432,512]{1,0:T(8,128)(2,1)S(1)}) custom-call(bf16[2048,512]{1,0:T(8,128)(2,1)S(1)} %copy-done, bf16[2064,128]{1,0:T(8,128)(2,1)S(1)} %get-tuple-element.17.after_ref, f32[3,257]{1,0:T(4,128)S(1)} %copy-done.1, ...), custom_call_target="tpu_custom_call" | custom-call | flops 1610612736 | bytes 4194304 | tf_op jit(solution)/shard_map/near_strip/pallas_call | solution.py:103
  5.3 4.1 %collective-permute-start.1 = (bf16[2064,128]{1,0:T(8,128)(2,1)S(1)}, bf16[2064,128]{1,0:T(8,128)(2,1)S(1)}, u32[]{:S(2)}, u32[]{:S(2)}) collective-permute-start(bf16[2064,128]{1,0:T(8,128)(2,1)S(1)} %get-tuple-element.24), channel_id=1, source_target_pairs={{0,32},{32,0},{64,96},{96,64},{128,160},{160,128},{192,224},{224,1... | collective-permute-start | bytes 1585160 | tf_op jit(solution)/shard_map/ppermute | solution.py:365
  9.5 0.0 copy-done.2
  9.5 0.0 copy-done.3
  9.5 0.0 copy-done.4
  9.5 0.0 copy-done.5
  9.5 0.0 copy-done.6
  9.5 0.9 %channel_tables.1 = (f32[8,2048]{1,0:T(8,128)S(1)}, bf16[160,2048]{1,0:T(8,128)(2,1)S(1)}, f32[24,128]{1,0:T(8,128)S(1)}) custom-call(f32[16]{0:T(128)S(1)} %copy-done.5, s32[5]{0:T(128)S(1)} %copy-done.6, f32[3,257]{1,0:T(4,128)S(1)} %copy-done.1, s32[3,2048]{1,0:T(4,128)S(1)} %bitcast.5, s32[512,128]{1,0:T(8,128)S(1)} %bitcast.3, s32[512,128]{1,0:T(8,128)S(1)} %bitcast.4), custom_call_target="tpu_custom_call" | custom-call | flops 1073741824 | bytes 1048576 | tf_op jit(solution)/shard_map/channel_tables/pallas_call | solution.py:234
  10.4 2.3 %inner_window.1.inner_ref = f32[160,256]{1,0:T(8,128)S(1)} custom-call(bf16[2048,512]{1,0:T(8,128)(2,1)S(1)} %copy-done, bf16[768,512]{1,0:T(8,128)(2,1)S(1)} %get-tuple-element.26.taps_ref, f32[8,2048]{1,0:T(8,128)S(1)} %get-tuple-element.22.gains_ref, bf16[160,2048]{1,0:T(8,128)(2,1)S(1)} %get-tuple-element.23.onehot_ref), custom_call_target="tpu_custom_call" | custom-call | flops 80530636800 | bytes 4194304 | tf_op jit(solution)/shard_map/inner_window/pallas_call | solution.py:316
  12.8 0.0 collective-permute-done.1.strip_ref
  12.8 1.6 %near_window.1.others_ref = f32[160,512]{1,0:T(8,128)S(1)} custom-call(bf16[2048,512]{1,0:T(8,128)(2,1)S(1)} %copy-done, bf16[2064,128]{1,0:T(8,128)(2,1)S(1)} %collective-permute-done.1.strip_ref, bf16[432,512]{1,0:T(8,128)(2,1)S(1)} %get-tuple-element.25.taps_ref, f32[8,2048]{1,0:T(8,128)S(1)} %get-tuple-element.22.gains_ref, ...), custom_call_target="tpu_custom_call" | custom-call | flops 1610612736 | bytes 4194304 | tf_op jit(solution)/shard_map/near_window/pallas_call | solution.py:316
  14.4 0.0 collective-permute-done.strip_ref
  14.4 1.7 %far_window.1 = bf16[32,24,128]{2,1,0:T(8,128)(2,1)S(1)} custom-call(bf16[2048,512]{1,0:T(8,128)(2,1)S(1)} %copy-done, bf16[2064,128]{1,0:T(8,128)(2,1)S(1)} %collective-permute-done.strip_ref, bf16[432,512]{1,0:T(8,128)(2,1)S(1)} %get-tuple-element.21.taps_ref, f32[8,2048]{1,0:T(8,128)S(1)} %get-tuple-element.22.gains_ref, ...), custom_call_target="tpu_custom_call" | custom-call | flops 1610612736 | bytes 4194304 | tf_op jit(solution)/shard_map/far_window/pallas_call | solution.py:316
  16.1 21.5 %all_to_all.5.parts_ref = bf16[32,24,128]{2,1,0:T(8,128)(2,1)S(1)} all-to-all(bf16[32,24,128]{2,1,0:T(8,128)(2,1)S(1)} %far_window.1), channel_id=1, replica_groups=mesh['tm'=16,'chan'=32] {'chan'}, dimensions={0} | all-to-all | bytes 393216 | tf_op jit(solution)/shard_map/all_to_all | solution.py:384
  37.7 0.7 %finish_sum.1 = f32[5,512]{1,0:T(8,128)} custom-call(f32[24,128]{1,0:T(8,128)S(1)} %get-tuple-element.16.divisor_ref, bf16[32,24,128]{2,1,0:T(8,128)(2,1)S(1)} %all_to_all.5.parts_ref), custom_call_target="tpu_custom_call" | custom-call | tf_op jit(solution)/shard_map/finish_sum/pallas_call | solution.py:342
Async XLA Ops:
  0.0 3.7 %copy-start = (bf16[2048,512]{1,0:T(8,128)(2,1)S(1)}, bf16[2048,512]{1,0:T(8,128)(2,1)}, u32[]{:S(2)}) copy-start(bf16[2048,512]{1,0:T(8,128)(2,1)} %raw_ref.9) | copy-start | bytes 6291460
  0.0 3.7 %copy-start.1 = (f32[3,257]{1,0:T(4,128)S(1)}, f32[3,257]{1,0:T(4,128)}, u32[]{:S(2)}) copy-start(f32[3,257]{1,0:T(4,128)} %taps_ref.5) | copy-start | bytes 9256
  1.5 12.9 %collective-permute-start = (bf16[2064,128]{1,0:T(8,128)(2,1)S(1)}, bf16[2064,128]{1,0:T(8,128)(2,1)S(1)}, u32[]{:S(2)}, u32[]{:S(2)}) collective-permute-start(bf16[2064,128]{1,0:T(8,128)(2,1)S(1)} %get-tuple-element.17.after_ref), channel_id=1, source_target_pairs={{32,64},{96,128},{160,192},{224,256},{288,320},{352,384},{416,448}... | collective-permute-start | bytes 1585160 | tf_op jit(solution)/shard_map/ppermute | solution.py:363
  3.8 5.7 %copy-start.2 = (s32[65536,1]{0,1:T(1,128)S(1)}, s32[65536,1]{0,1:T(1,128)}, u32[]{:S(2)}) copy-start(s32[65536,1]{0,1:T(1,128)} %param.11) | copy-start | bytes 786436
  3.8 5.7 %copy-start.3 = (s32[65536]{0:T(1024)S(1)}, s32[65536]{0:T(1024)}, u32[]{:S(2)}) copy-start(s32[65536]{0:T(1024)} %param.12) | copy-start | bytes 786436
  3.8 5.7 %copy-start.4 = (s32[2048,3]{0,1:T(4,128)S(1)}, s32[2048,3]{0,1:T(4,128)}, u32[]{:S(2)}) copy-start(s32[2048,3]{0,1:T(4,128)} %param.10) | copy-start | bytes 73732
  3.8 5.7 %copy-start.5 = (f32[16]{0:T(128)S(1)}, f32[16]{0:T(128)}, u32[]{:S(2)}) copy-start(f32[16]{0:T(128)} %levels_ref.1) | copy-start | bytes 196
  3.8 5.7 %copy-start.6 = (s32[5]{0:T(128)S(1)}, s32[5]{0:T(128)}, u32[]{:S(2)}) copy-start(s32[5]{0:T(128)} %length_ref.1) | copy-start | bytes 64
  5.3 7.4 %collective-permute-start.1 = (bf16[2064,128]{1,0:T(8,128)(2,1)S(1)}, bf16[2064,128]{1,0:T(8,128)(2,1)S(1)}, u32[]{:S(2)}, u32[]{:S(2)}) collective-permute-start(bf16[2064,128]{1,0:T(8,128)(2,1)S(1)} %get-tuple-element.24), channel_id=1, source_target_pairs={{0,32},{32,0},{64,96},{96,64},{128,160},{160,128},{192,224},{224,1... | collective-permute-start | bytes 1585160 | tf_op jit(solution)/shard_map/ppermute | solution.py:365

commit v4 on v3

--- a/solution.py
+++ b/solution.py
@@ -199,8 +199,9 @@
     return [jax.ShapeDtypeStruct((taps.shape[0] * r, depth), BF16) for r in rows]
 
 
-def channels_kernel(
-    levels_ref, length_ref, taps_ref, index_ref, owner_ref, seat_ref, gains_ref, onehot_ref, divisor_ref
+def inner_kernel(
+    levels_ref, length_ref, raw_ref, inner_taps_ref, taps_ref, index_ref, owner_ref, seat_ref,
+    sums_ref, gains_ref, onehot_ref, divisor_ref,
 ):
     is_low = is_low_core()
     bands, width = taps_ref.shape
@@ -226,30 +227,9 @@
     divisor_ref[...] = jnp.ones_like(divisor_ref)
     for k in range(length_ref.shape[0]):
         divisor_ref[k * tiles : (k + 1) * tiles, :] = jnp.full((tiles, LANES), length_ref[k].astype(F32))
-
-
-def channel_tables(band_gain, cable_length, taps, index, owner, seat, cables, pitch):
-    count = index.shape[1]
-    vmem = pl.BlockSpec(memory_space=pltpu.VMEM)
-    return pl.pallas_call(
-        channels_kernel,
-        in_specs=[pl.BlockSpec(memory_space=pltpu.SMEM)] * 2 + [vmem] * 4,
-        out_specs=[vmem] * 3,
-        out_shape=[
-            jax.ShapeDtypeStruct((8, count), F32),
-            jax.ShapeDtypeStruct((cables, count), BF16),
-            jax.ShapeDtypeStruct((pitch, LANES), F32),
-        ],
-        compiler_params=pltpu.CompilerParams(vmem_limit_bytes=8 << 20),
-        cost_estimate=pl.CostEstimate(flops=1 << 30, bytes_accessed=1 << 20, transcendentals=0),
-        name="channel_tables",
-    )(band_gain, cable_length, taps, index, owner, seat)
-
-
-def inner_kernel(raw_ref, taps_ref, gains_ref, onehot_ref, sums_ref):
     count = raw_ref.shape[0]
     sums_ref[...] = window_sums(
-        lambda part: raw_ref[part, :], taps_ref, INNER, gains_ref, None, onehot_ref, count, INNER_COLS
+        lambda part: raw_ref[part, :], inner_taps_ref, INNER, gains_ref, None, onehot_ref, count, INNER_COLS
     )
 
 
@@ -310,21 +290,20 @@
         out_ref[o, :, :] = scr[o * pitch : (o + 1) * pitch, :].astype(BF16)
 
 
-def window(kernel, name, out_shape, scratch, taps_at, args):
-    count, depth = args[0].shape
+def window(kernel, name, out_shape, scratch, flops, args, scalars=()):
+    smem = pl.BlockSpec(memory_space=pltpu.SMEM)
     vmem = pl.BlockSpec(memory_space=pltpu.VMEM)
+    many = isinstance(out_shape, list)
     return pl.pallas_call(
         kernel,
-        in_specs=[vmem] * len(args),
-        out_specs=vmem,
+        in_specs=[smem] * len(scalars) + [vmem] * len(args),
+        out_specs=[vmem] * len(out_shape) if many else vmem,
         out_shape=out_shape,
         scratch_shapes=scratch,
         compiler_params=pltpu.CompilerParams(vmem_limit_bytes=24 << 20),
-        cost_estimate=pl.CostEstimate(
-            flops=(50 if name == 'inner_window' else 1) * 2 * count * depth * 768, bytes_accessed=4<<20, transcendentals=0
-        ),
+        cost_estimate=pl.CostEstimate(flops=flops, bytes_accessed=4 << 20, transcendentals=0),
         name=name,
-    )(*args)
+    )(*scalars, *args)
 
 
 def finish_kernel(divisor_ref, parts_ref, out_ref):
@@ -364,21 +343,29 @@
     near_sent, inner_taps, far_taps, near_taps = near_pack(raw, far_sent, band_taps, early)
     near_strip = lax.ppermute(near_sent, "tm", near_pairs)
     pitch = -(-(depth // LANES) * cab_dev // 8) * 8
-    gains, onehot, divisor = channel_tables(
-        band_gain, cable_length, band_taps, gain_index.T,
-        owner_of.reshape(-1, LANES), seat.reshape(-1, LANES), cables, pitch,
-    )
-    inner_sums = window(
-        inner_kernel, "inner_window", jax.ShapeDtypeStruct((cables, INNER), F32), [], 1,
-        (raw, inner_taps, gains, onehot),
+    work = 2 * raw.shape[0] * depth * inner_taps.shape[0]
+    inner_sums, gains, onehot, divisor = window(
+        inner_kernel, "inner_window",
+        [
+            jax.ShapeDtypeStruct((cables, INNER), F32),
+            jax.ShapeDtypeStruct((8, raw.shape[0]), F32),
+            jax.ShapeDtypeStruct((cables, raw.shape[0]), BF16),
+            jax.ShapeDtypeStruct((pitch, LANES), F32),
+        ],
+        [], 50 * work,
+        (
+            raw, inner_taps, band_taps, gain_index.T,
+            owner_of.reshape(-1, LANES), seat.reshape(-1, LANES),
+        ),
+        (band_gain, cable_length),
     )
     others = window(
-        near_kernel, "near_window", jax.ShapeDtypeStruct((cables, depth), F32), [], 2,
+        near_kernel, "near_window", jax.ShapeDtypeStruct((cables, depth), F32), [], work,
         (raw, near_strip, near_taps, gains, onehot, inner_sums),
     )
     parts = window(
         far_kernel, "far_window", jax.ShapeDtypeStruct((chan_count, pitch, LANES), BF16),
-        [pltpu.VMEM((chan_count * pitch, LANES), F32)], 2,
+        [pltpu.VMEM((chan_count * pitch, LANES), F32)], work,
         (raw, far_strip, far_taps, gains, onehot, others),
     )
     parts = lax.all_to_all(parts, "chan", split_axis=0, concat_axis=0, tiled=True)

time: 38.5 us -> 38.3 us (level)
    pallas_call x4 -> x3, Pallas kernels: 6.53 us -> 6.26 us  [window(): pl.pallas_call(kernel, in_specs=[smem] * len(scalars) + [vmem] * len(args...]
  transfers between devices with their start and end apart: 2 -> 2, of which waited for: 0 -> 0; matrix products, arithmetic and copies ran while one was open for 0% -> 0% of each run, Pallas kernels for 17% -> 16%
where the time goes in v4:
time: 38.3 us; the launch traced here: 38.1 us
  blocking collectives  21.6 us (56%)
  Pallas kernels  9.9 us (26%)
  starting transfers between devices  6.38 us (17%)
    all_to_all x1, blocking collectives, shards(): lax.all_to_all(parts, 'chan', split_axis=0, concat_axis=0, tiled=True)  21.6 us
    pallas_call x3, Pallas kernels, window(): pl.pallas_call(kernel, in_specs=[smem] * len(scalars) + [vmem] * len(args...  6.26 us
    ppermute x1, starting transfers between devices, shards(): near_strip = lax.ppermute(near_sent, 'tm', near_pairs)  4.15 us
    ppermute x1, starting transfers between devices, shards(): far_strip = lax.ppermute(far_sent, 'tm', far_pairs)  2.24 us
    pallas_call x1, Pallas kernels, near_pack(): pl.pallas_call(near_pack_kernel, in_specs=[vmem, pl.BlockSpec(memory_spac...  1.51 us
    pallas_call x1, Pallas kernels, first(): pl.pallas_call(first_kernel, in_specs=[pl.BlockSpec(memory_space=pltpu.HB...  1.47 us
  transfers between devices with their start and end apart: 2, of which 0 were waited for; matrix products, arithmetic and copies ran while one was open for 0% of the time, Pallas kernels for 16%

profile of v4, /device:TPU:192, one launch (start us, length us, event | category | flops | bytes accessed | tf_op | source)
XLA Modules:
  0.0 38.1 jit_solution(6779085208482916196)
XLA Ops:
  0.0 0.0 copy-start
  0.0 0.0 copy-start.1
  0.0 1.5 %far_strip.1 = (bf16[2064,128]{1,0:T(8,128)(2,1)S(1)}, bf16[768,512]{1,0:T(8,128)(2,1)S(1)}, bf16[432,512]{1,0:T(8,128)(2,1)S(1)}, bf16[432,512]{1,0:T(8,128)(2,1)S(1)}) custom-call(bf16[2048,512]{1,0:T(8,128)(2,1)} %raw_ref.9, f32[3,257]{1,0:T(4,128)} %taps_ref.5), custom_call_target="tpu_custom_call" | custom-call | tf_op jit(solution)/shard_map/far_strip/pallas_call | solution.py:85
  1.5 2.2 %collective-permute-start = (bf16[2064,128]{1,0:T(8,128)(2,1)S(1)}, bf16[2064,128]{1,0:T(8,128)(2,1)S(1)}, u32[]{:S(2)}, u32[]{:S(2)}) collective-permute-start(bf16[2064,128]{1,0:T(8,128)(2,1)S(1)} %get-tuple-element.17.after_ref), channel_id=1, source_target_pairs={{32,64},{96,128},{160,192},{224,256},{288,320},{352,384},{416,448}... | collective-permute-start | bytes 1585160 | tf_op jit(solution)/shard_map/ppermute | solution.py:342
  3.7 0.0 copy-done
  3.7 0.0 copy-done.1
  3.8 0.0 copy-start.2
  3.8 0.0 copy-start.3
  3.8 0.0 copy-start.4
  3.8 0.0 copy-start.5
  3.8 0.0 copy-start.6
  3.8 1.5 %near_strip.1 = (bf16[2064,128]{1,0:T(8,128)(2,1)S(1)}, bf16[768,512]{1,0:T(8,128)(2,1)S(1)}, bf16[432,512]{1,0:T(8,128)(2,1)S(1)}, bf16[432,512]{1,0:T(8,128)(2,1)S(1)}) custom-call(bf16[2048,512]{1,0:T(8,128)(2,1)S(1)} %copy-done, bf16[2064,128]{1,0:T(8,128)(2,1)S(1)} %get-tuple-element.17.after_ref, f32[3,257]{1,0:T(4,128)S(1)} %copy-done.1, ...), custom_call_target="tpu_custom_call" | custom-call | flops 1610612736 | bytes 4194304 | tf_op jit(solution)/shard_map/near_strip/pallas_call | solution.py:103
  5.3 4.1 %collective-permute-start.1 = (bf16[2064,128]{1,0:T(8,128)(2,1)S(1)}, bf16[2064,128]{1,0:T(8,128)(2,1)S(1)}, u32[]{:S(2)}, u32[]{:S(2)}) collective-permute-start(bf16[2064,128]{1,0:T(8,128)(2,1)S(1)} %get-tuple-element.26), channel_id=1, source_target_pairs={{0,32},{32,0},{64,96},{96,64},{128,160},{160,128},{192,224},{224,1... | collective-permute-start | bytes 1585160 | tf_op jit(solution)/shard_map/ppermute | solution.py:344
  9.5 0.0 copy-done.2
  9.5 0.0 copy-done.3
  9.5 0.0 copy-done.4
  9.5 0.0 copy-done.5
  9.5 0.0 copy-done.6
  9.5 3.0 %inner_window.1 = (f32[160,256]{1,0:T(8,128)S(1)}, f32[8,2048]{1,0:T(8,128)S(1)}, bf16[160,2048]{1,0:T(8,128)(2,1)S(1)}, f32[24,128]{1,0:T(8,128)S(1)}) custom-call(f32[16]{0:T(128)S(1)} %copy-done.5, s32[5]{0:T(128)S(1)} %copy-done.6, bf16[2048,512]{1,0:T(8,128)(2,1)S(1)} %copy-done, bf16[768,512]{1,0:T(8,128)(2,1)S(1)} %get-tuple-element.21.inner_taps_ref, ...), custom_call_target="tpu_custom_call" | custom-call | flops 80530636800 | bytes 4194304 | tf_op jit(solution)/shard_map/inner_window/pallas_call | solution.py:297
  12.5 0.0 collective-permute-done.1.strip_ref
  12.5 1.6 %near_window.1.others_ref = f32[160,512]{1,0:T(8,128)S(1)} custom-call(bf16[2048,512]{1,0:T(8,128)(2,1)S(1)} %copy-done, bf16[2064,128]{1,0:T(8,128)(2,1)S(1)} %collective-permute-done.1.strip_ref, bf16[432,512]{1,0:T(8,128)(2,1)S(1)} %get-tuple-element.27.taps_ref, f32[8,2048]{1,0:T(8,128)S(1)} %get-tuple-element.24.gains_ref, ...), custom_call_target="tpu_custom_call" | custom-call | flops 1610612736 | bytes 4194304 | tf_op jit(solution)/shard_map/near_window/pallas_call | solution.py:297
  14.1 0.0 collective-permute-done.strip_ref
  14.2 1.7 %far_window.1 = bf16[32,24,128]{2,1,0:T(8,128)(2,1)S(1)} custom-call(bf16[2048,512]{1,0:T(8,128)(2,1)S(1)} %copy-done, bf16[2064,128]{1,0:T(8,128)(2,1)S(1)} %collective-permute-done.strip_ref, bf16[432,512]{1,0:T(8,128)(2,1)S(1)} %get-tuple-element.23.taps_ref, f32[8,2048]{1,0:T(8,128)S(1)} %get-tuple-element.24.gains_ref, ...), custom_call_target="tpu_custom_call" | custom-call | flops 1610612736 | bytes 4194304 | tf_op jit(solution)/shard_map/far_window/pallas_call | solution.py:297
  15.8 21.6 %all_to_all.5.parts_ref = bf16[32,24,128]{2,1,0:T(8,128)(2,1)S(1)} all-to-all(bf16[32,24,128]{2,1,0:T(8,128)(2,1)S(1)} %far_window.1), channel_id=1, replica_groups=mesh['tm'=16,'chan'=32] {'chan'}, dimensions={0} | all-to-all | bytes 393216 | tf_op jit(solution)/shard_map/all_to_all | solution.py:371
  37.5 0.7 %finish_sum.1 = f32[5,512]{1,0:T(8,128)} custom-call(f32[24,128]{1,0:T(8,128)S(1)} %get-tuple-element.22.divisor_ref, bf16[32,24,128]{2,1,0:T(8,128)(2,1)S(1)} %all_to_all.5.parts_ref), custom_call_target="tpu_custom_call" | custom-call | tf_op jit(solution)/shard_map/finish_sum/pallas_call | solution.py:321
Async XLA Ops:
  0.0 3.7 %copy-start = (bf16[2048,512]{1,0:T(8,128)(2,1)S(1)}, bf16[2048,512]{1,0:T(8,128)(2,1)}, u32[]{:S(2)}) copy-start(bf16[2048,512]{1,0:T(8,128)(2,1)} %raw_ref.9) | copy-start | bytes 6291460
  0.0 3.7 %copy-start.1 = (f32[3,257]{1,0:T(4,128)S(1)}, f32[3,257]{1,0:T(4,128)}, u32[]{:S(2)}) copy-start(f32[3,257]{1,0:T(4,128)} %taps_ref.5) | copy-start | bytes 9256
  1.5 12.7 %collective-permute-start = (bf16[2064,128]{1,0:T(8,128)(2,1)S(1)}, bf16[2064,128]{1,0:T(8,128)(2,1)S(1)}, u32[]{:S(2)}, u32[]{:S(2)}) collective-permute-start(bf16[2064,128]{1,0:T(8,128)(2,1)S(1)} %get-tuple-element.17.after_ref), channel_id=1, source_target_pairs={{32,64},{96,128},{160,192},{224,256},{288,320},{352,384},{416,448}... | collective-permute-start | bytes 1585160 | tf_op jit(solution)/shard_map/ppermute | solution.py:342
  3.8 5.7 %copy-start.2 = (s32[65536,1]{0,1:T(1,128)S(1)}, s32[65536,1]{0,1:T(1,128)}, u32[]{:S(2)}) copy-start(s32[65536,1]{0,1:T(1,128)} %param.11) | copy-start | bytes 786436
  3.8 5.7 %copy-start.3 = (s32[65536]{0:T(1024)S(1)}, s32[65536]{0:T(1024)}, u32[]{:S(2)}) copy-start(s32[65536]{0:T(1024)} %param.12) | copy-start | bytes 786436
  3.8 5.7 %copy-start.4 = (s32[2048,3]{0,1:T(4,128)S(1)}, s32[2048,3]{0,1:T(4,128)}, u32[]{:S(2)}) copy-start(s32[2048,3]{0,1:T(4,128)} %param.10) | copy-start | bytes 73732
  3.8 5.7 %copy-start.5 = (f32[16]{0:T(128)S(1)}, f32[16]{0:T(128)}, u32[]{:S(2)}) copy-start(f32[16]{0:T(128)} %levels_ref.1) | copy-start | bytes 196
  3.8 5.7 %copy-start.6 = (s32[5]{0:T(128)S(1)}, s32[5]{0:T(128)}, u32[]{:S(2)}) copy-start(s32[5]{0:T(128)} %length_ref.1) | copy-start | bytes 64
  5.3 7.2 %collective-permute-start.1 = (bf16[2064,128]{1,0:T(8,128)(2,1)S(1)}, bf16[2064,128]{1,0:T(8,128)(2,1)S(1)}, u32[]{:S(2)}, u32[]{:S(2)}) collective-permute-start(bf16[2064,128]{1,0:T(8,128)(2,1)S(1)} %get-tuple-element.26), channel_id=1, source_target_pairs={{0,32},{32,0},{64,96},{96,64},{128,160},{160,128},{192,224},{224,1... | collective-permute-start | bytes 1585160 | tf_op jit(solution)/shard_map/ppermute | solution.py:344

commit v5 on v4

--- a/solution.py
+++ b/solution.py
@@ -113,15 +113,23 @@
     )(raw, after, taps, *early)
 
 
-def window_sums(columns_of, taps_ref, size, gains_ref, edges_of, onehot_ref, count, step):
+def combined(taps, columns, size, gains_ref, part):
+    bands = lax.dot_general(taps, columns, NT, preferred_element_type=F32)
+    held = gains_ref[0:1, part] * bands[0:size]
+    for b in (1, 2):
+        held = held + gains_ref[b : b + 1, part] * bands[b * size : (b + 1) * size]
+    return held
+
+
+def window_sums(columns_of, taps_ref, size, gains_ref, edges_of, onehot_ref, count, step, own_ref=None):
     sub = lax.broadcasted_iota(jnp.int32, (8, step), 0)
     total = None
     for start in range(0, count, step):
         part = slice(start, start + step)
-        bands = lax.dot_general(taps_ref[...], columns_of(part), NT, preferred_element_type=F32)
-        held = gains_ref[0:1, part] * bands[0:size]
-        for b in (1, 2):
-            held = held + gains_ref[b : b + 1, part] * bands[b * size : (b + 1) * size]
+        columns = columns_of(part)
+        held = combined(taps_ref[:, 0 : columns.shape[1]], columns, size, gains_ref, part)
+        if own_ref is not None:
+            held = held + own_ref[:, part]
         first, last = held[0:8], held[size - 8 : size]
         if edges_of is not None:
             low, high = edges_of(start)
@@ -208,8 +216,8 @@
     blocks = index_ref.shape[1] // LANES
     index = index_ref[...]
     gains = jnp.zeros(index.shape, F32)
-    for level in range(levels_ref.shape[0]):
-        gains = jnp.where(index == level, levels_ref[level], gains)
+    for level in range(levels_ref.shape[1]):
+        gains = jnp.where(index == level, levels_ref[:, level : level + 1], gains)
     gains = 0.5 * gains
     first = taps_ref[:, 0:1].astype(BF16).astype(F32)
     final = taps_ref[:, width - 1 : width].astype(BF16).astype(F32)
@@ -223,22 +231,26 @@
     cable = lax.broadcasted_iota(jnp.int32, (onehot_ref.shape[0], LANES), 0)
     for a in range(blocks):
         onehot_ref[:, a * LANES : (a + 1) * LANES] = (cable == place[a : a + 1, :]).astype(F32).astype(BF16)
-    tiles = divisor_ref.shape[0] // length_ref.shape[0]
+    tiles = divisor_ref.shape[0] // length_ref.shape[1]
     divisor_ref[...] = jnp.ones_like(divisor_ref)
-    for k in range(length_ref.shape[0]):
-        divisor_ref[k * tiles : (k + 1) * tiles, :] = jnp.full((tiles, LANES), length_ref[k].astype(F32))
+    for k in range(length_ref.shape[1]):
+        divisor_ref[k * tiles : (k + 1) * tiles, :] = jnp.broadcast_to(
+            length_ref[:, k : k + 1].astype(F32), (tiles, LANES)
+        )
     count = raw_ref.shape[0]
     sums_ref[...] = window_sums(
         lambda part: raw_ref[part, :], inner_taps_ref, INNER, gains_ref, None, onehot_ref, count, INNER_COLS
     )
 
 
-def side_sums(is_low, edge_row, raw_ref, strip_ref, taps_ref, gains_ref, onehot_ref):
-    count = raw_ref.shape[0]
+def side_sums(is_low, edge_row, raw_ref, strip_ref, taps_ref, gains_ref, onehot_ref, own_ref=None):
+    count = strip_ref.shape[0] - 16
     offset = pl.multiple_of(jnp.where(is_low, 0, LANES), LANES)
     beside = strip_ref[count:, :].astype(F32)
 
     def columns_of(part):
+        if own_ref is not None:
+            return strip_ref[part, :]
         return jnp.concatenate([strip_ref[part, :], raw_ref[part, pl.ds(offset, 3 * LANES)]], axis=1)
 
     def edges_of(start):
@@ -248,9 +260,9 @@
         return jnp.where(is_low, line, 0.0), jnp.where(is_low, 0.0, line)
 
     sums = window_sums(
-        columns_of, taps_ref, SIDE, gains_ref, edges_of, onehot_ref, count, SIDE_COLS
-    )
-    depth = raw_ref.shape[1]
+        columns_of, taps_ref, SIDE, gains_ref, edges_of, onehot_ref, count, SIDE_COLS, own_ref
+    )
+    depth = taps_ref.shape[1]
     sample = sample_of_row(SIDE, SIDE, depth)
     sample = sample + jnp.where(is_low, -1, depth + 1 - SIDE)
     kept = (sample >= jnp.where(is_low, 0, depth - 1 - LANES)) & (
@@ -261,7 +273,15 @@
     return jnp.dot(sums.astype(BF16), order, preferred_element_type=F32)
 
 
-def near_kernel(raw_ref, strip_ref, taps_ref, gains_ref, onehot_ref, inner_ref, sums_ref):
+def near_kernel(
+    raw_ref, strip_ref, taps_ref, gains_ref, onehot_ref, inner_ref, far_taps_ref, sums_ref, own_ref
+):
+    count = raw_ref.shape[0]
+    offset = pl.multiple_of(jnp.where(is_low_core(), 0, LANES), LANES)
+    for start in range(0, count, SIDE_COLS):
+        part = slice(start, start + SIDE_COLS)
+        columns = raw_ref[part, pl.ds(offset, 3 * LANES)]
+        own_ref[:, part] = combined(far_taps_ref[:, LANES:], columns, SIDE, gains_ref, part)
     near = side_sums(jnp.logical_not(is_low_core()), 4, raw_ref, strip_ref, taps_ref, gains_ref, onehot_ref)
     depth = raw_ref.shape[1]
     sample = sample_of_row(INNER, INNER, depth) + LANES
@@ -271,12 +291,10 @@
     sums_ref[...] = near + jnp.dot(inner_ref[...].astype(BF16), order, preferred_element_type=F32)
 
 
-def far_kernel(
-    raw_ref, strip_ref, taps_ref, gains_ref, onehot_ref, others_ref, out_ref, scr
-):
+def far_kernel(strip_ref, taps_ref, gains_ref, onehot_ref, others_ref, own_ref, out_ref, scr):
     owners, pitch, _ = out_ref.shape
     seats = others_ref.shape[0] // owners
-    far = side_sums(is_low_core(), 3, raw_ref, strip_ref, taps_ref, gains_ref, onehot_ref)
+    far = side_sums(is_low_core(), 3, None, strip_ref, taps_ref, gains_ref, onehot_ref, own_ref)
     sums = others_ref[...] + far
     tiles = sums.shape[1] // LANES
     for spare in range(tiles * seats, pitch):
@@ -290,20 +308,19 @@
         out_ref[o, :, :] = scr[o * pitch : (o + 1) * pitch, :].astype(BF16)
 
 
-def window(kernel, name, out_shape, scratch, flops, args, scalars=()):
-    smem = pl.BlockSpec(memory_space=pltpu.SMEM)
+def window(kernel, name, out_shape, scratch, flops, args):
     vmem = pl.BlockSpec(memory_space=pltpu.VMEM)
     many = isinstance(out_shape, list)
     return pl.pallas_call(
         kernel,
-        in_specs=[smem] * len(scalars) + [vmem] * len(args),
+        in_specs=[vmem] * len(args),
         out_specs=[vmem] * len(out_shape) if many else vmem,
         out_shape=out_shape,
         scratch_shapes=scratch,
         compiler_params=pltpu.CompilerParams(vmem_limit_bytes=24 << 20),
         cost_estimate=pl.CostEstimate(flops=flops, bytes_accessed=4 << 20, transcendentals=0),
         name=name,
-    )(*scalars, *args)
+    )(*args)
 
 
 def finish_kernel(divisor_ref, parts_ref, out_ref):
@@ -354,19 +371,19 @@
         ],
         [], 50 * work,
         (
-            raw, inner_taps, band_taps, gain_index.T,
-            owner_of.reshape(-1, LANES), seat.reshape(-1, LANES),
+            band_gain.reshape(1, -1), cable_length.reshape(1, -1), raw, inner_taps, band_taps,
+            gain_index.T, owner_of.reshape(-1, LANES), seat.reshape(-1, LANES),
         ),
-        (band_gain, cable_length),
-    )
-    others = window(
-        near_kernel, "near_window", jax.ShapeDtypeStruct((cables, depth), F32), [], work,
-        (raw, near_strip, near_taps, gains, onehot, inner_sums),
+    )
+    others, own = window(
+        near_kernel, "near_window",
+        [jax.ShapeDtypeStruct((cables, depth), F32), jax.ShapeDtypeStruct((SIDE, raw.shape[0]), F32)],
+        [], work, (raw, near_strip, near_taps, gains, onehot, inner_sums, far_taps),
     )
     parts = window(
         far_kernel, "far_window", jax.ShapeDtypeStruct((chan_count, pitch, LANES), BF16),
         [pltpu.VMEM((chan_count * pitch, LANES), F32)], work,
-        (raw, far_strip, far_taps, gains, onehot, others),
+        (far_strip, far_taps, gains, onehot, others, own),
     )
     parts = lax.all_to_all(parts, "chan", split_axis=0, concat_axis=0, tiled=True)
     return finish(parts, divisor, cab_dev, depth)

time: 38.3 us -> 38.1 us (level)
  transfers between devices with their start and end apart: 2 -> 2, of which waited for: 0 -> 0; matrix products, arithmetic and copies ran while one was open for 0% -> 0% of each run, Pallas kernels for 16% -> 17%
where the time goes in v5:
time: 38.1 us; the launch traced here: 37.9 us
  blocking collectives  21.5 us (56%)
  Pallas kernels  9.81 us (26%)
  starting transfers between devices  6.38 us (17%)
    all_to_all x1, blocking collectives, shards(): lax.all_to_all(parts, 'chan', split_axis=0, concat_axis=0, tiled=True)  21.5 us
    pallas_call x3, Pallas kernels, window(): pl.pallas_call(kernel, in_specs=[vmem] * len(args), out_specs=[vmem] * le...  6.17 us
    ppermute x1, starting transfers between devices, shards(): near_strip = lax.ppermute(near_sent, 'tm', near_pairs)  4.15 us
    ppermute x1, starting transfers between devices, shards(): far_strip = lax.ppermute(far_sent, 'tm', far_pairs)  2.24 us
    pallas_call x1, Pallas kernels, near_pack(): pl.pallas_call(near_pack_kernel, in_specs=[vmem, pl.BlockSpec(memory_spac...  1.51 us
    pallas_call x1, Pallas kernels, first(): pl.pallas_call(first_kernel, in_specs=[pl.BlockSpec(memory_space=pltpu.HB...  1.47 us
  transfers between devices with their start and end apart: 2, of which 0 were waited for; matrix products, arithmetic and copies ran while one was open for 0% of the time, Pallas kernels for 17%

profile of v5, /device:TPU:192, one launch (start us, length us, event | category | flops | bytes accessed | tf_op | source)
XLA Modules:
  0.0 37.9 jit_solution(4378235519313834592)
XLA Ops:
  0.0 0.0 copy-start
  0.0 0.0 copy-start.1
  0.0 1.5 %far_strip.1 = (bf16[2064,128]{1,0:T(8,128)(2,1)S(1)}, bf16[768,512]{1,0:T(8,128)(2,1)S(1)}, bf16[432,512]{1,0:T(8,128)(2,1)S(1)}, bf16[432,512]{1,0:T(8,128)(2,1)S(1)}) custom-call(bf16[2048,512]{1,0:T(8,128)(2,1)} %raw_ref.7, f32[3,257]{1,0:T(4,128)} %taps_ref.5), custom_call_target="tpu_custom_call" | custom-call | tf_op jit(solution)/shard_map/far_strip/pallas_call | solution.py:85
  1.5 2.2 %collective-permute-start = (bf16[2064,128]{1,0:T(8,128)(2,1)S(1)}, bf16[2064,128]{1,0:T(8,128)(2,1)S(1)}, u32[]{:S(2)}, u32[]{:S(2)}) collective-permute-start(bf16[2064,128]{1,0:T(8,128)(2,1)S(1)} %get-tuple-element.19.after_ref), channel_id=1, source_target_pairs={{32,64},{96,128},{160,192},{224,256},{288,320},{352,384},{416,448}... | collective-permute-start | bytes 1585160 | tf_op jit(solution)/shard_map/ppermute | solution.py:359
  3.7 0.0 copy-done
  3.7 0.0 copy-done.1
  3.8 0.0 copy-start.2
  3.8 0.0 copy-start.3
  3.8 0.0 copy-start.4
  3.8 0.0 copy-start.5
  3.8 0.0 copy-start.6
  3.8 1.5 %near_strip.1 = (bf16[2064,128]{1,0:T(8,128)(2,1)S(1)}, bf16[768,512]{1,0:T(8,128)(2,1)S(1)}, bf16[432,512]{1,0:T(8,128)(2,1)S(1)}, bf16[432,512]{1,0:T(8,128)(2,1)S(1)}) custom-call(bf16[2048,512]{1,0:T(8,128)(2,1)S(1)} %copy-done, bf16[2064,128]{1,0:T(8,128)(2,1)S(1)} %get-tuple-element.19.after_ref, f32[3,257]{1,0:T(4,128)S(1)} %copy-done.1, ...), custom_call_target="tpu_custom_call" | custom-call | flops 1610612736 | bytes 4194304 | tf_op jit(solution)/shard_map/near_strip/pallas_call | solution.py:103
  5.3 4.1 %collective-permute-start.1 = (bf16[2064,128]{1,0:T(8,128)(2,1)S(1)}, bf16[2064,128]{1,0:T(8,128)(2,1)S(1)}, u32[]{:S(2)}, u32[]{:S(2)}) collective-permute-start(bf16[2064,128]{1,0:T(8,128)(2,1)S(1)} %get-tuple-element.28), channel_id=1, source_target_pairs={{0,32},{32,0},{64,96},{96,64},{128,160},{160,128},{192,224},{224,1... | collective-permute-start | bytes 1585160 | tf_op jit(solution)/shard_map/ppermute | solution.py:361
  9.5 0.0 copy-done.2
  9.5 0.0 copy-done.3
  9.5 0.0 copy-done.4
  9.5 0.0 copy-done.5
  9.5 0.0 copy-done.6
  9.5 2.4 %inner_window.1 = (f32[160,256]{1,0:T(8,128)S(1)}, f32[8,2048]{1,0:T(8,128)S(1)}, bf16[160,2048]{1,0:T(8,128)(2,1)S(1)}, f32[24,128]{1,0:T(8,128)S(1)}) custom-call(f32[1,16]{1,0:T(1,128)S(1)} %bitcast.8, s32[1,5]{1,0:T(1,128)S(1)} %bitcast.9, bf16[2048,512]{1,0:T(8,128)(2,1)S(1)} %copy-done, bf16[768,512]{1,0:T(8,128)(2,1)S(1)} %get-tuple-element.23.inner_taps_ref, ...), custom_call_target="tpu_custom_call" | custom-call | flops 80530636800 | bytes 4194304 | tf_op jit(solution)/shard_map/inner_window/pallas_call | solution.py:314
  12.0 0.0 collective-permute-done.1.strip_ref
  12.0 2.6 %near_window.1 = (f32[160,512]{1,0:T(8,128)S(1)}, f32[144,2048]{1,0:T(8,128)S(1)}) custom-call(bf16[2048,512]{1,0:T(8,128)(2,1)S(1)} %copy-done, bf16[2064,128]{1,0:T(8,128)(2,1)S(1)} %collective-permute-done.1.strip_ref, bf16[432,512]{1,0:T(8,128)(2,1)S(1)} %get-tuple-element.29.taps_ref, f32[8,2048]{1,0:T(8,128)S(1)} %get-tuple-element.26.gains_ref, ...), custom_call_target="tpu_custom_call" | custom-call | flops 1610612736 | bytes 4194304 | tf_op jit(solution)/shard_map/near_window/pallas_call | solution.py:314
  14.6 0.0 collective-permute-done.strip_ref
  14.6 1.2 %far_window.1 = bf16[32,24,128]{2,1,0:T(8,128)(2,1)S(1)} custom-call(bf16[2064,128]{1,0:T(8,128)(2,1)S(1)} %collective-permute-done.strip_ref, bf16[432,512]{1,0:T(8,128)(2,1)S(1)} %get-tuple-element.25.far_taps_ref.taps_ref, f32[8,2048]{1,0:T(8,128)S(1)} %get-tuple-element.26.gains_ref, bf16[160,2048]{1,0:T(8,128)(2,1)S(1)} %get-tuple-element.27.onehot_ref, ...), custom_call_target="tpu_custom_call" | custom-call | flops 1610612736 | bytes 4194304 | tf_op jit(solution)/shard_map/far_window/pallas_call | solution.py:314
  15.7 21.5 %all_to_all.5.parts_ref = bf16[32,24,128]{2,1,0:T(8,128)(2,1)S(1)} all-to-all(bf16[32,24,128]{2,1,0:T(8,128)(2,1)S(1)} %far_window.1), channel_id=1, replica_groups=mesh['tm'=16,'chan'=32] {'chan'}, dimensions={0} | all-to-all | bytes 393216 | tf_op jit(solution)/shard_map/all_to_all | solution.py:388
  37.3 0.7 %finish_sum.1 = f32[5,512]{1,0:T(8,128)} custom-call(f32[24,128]{1,0:T(8,128)S(1)} %get-tuple-element.24.divisor_ref, bf16[32,24,128]{2,1,0:T(8,128)(2,1)S(1)} %all_to_all.5.parts_ref), custom_call_target="tpu_custom_call" | custom-call | tf_op jit(solution)/shard_map/finish_sum/pallas_call | solution.py:338
Async XLA Ops:
  0.0 3.7 %copy-start = (bf16[2048,512]{1,0:T(8,128)(2,1)S(1)}, bf16[2048,512]{1,0:T(8,128)(2,1)}, u32[]{:S(2)}) copy-start(bf16[2048,512]{1,0:T(8,128)(2,1)} %raw_ref.7) | copy-start | bytes 6291460
  0.0 3.7 %copy-start.1 = (f32[3,257]{1,0:T(4,128)S(1)}, f32[3,257]{1,0:T(4,128)}, u32[]{:S(2)}) copy-start(f32[3,257]{1,0:T(4,128)} %taps_ref.5) | copy-start | bytes 9256
  1.5 13.1 %collective-permute-start = (bf16[2064,128]{1,0:T(8,128)(2,1)S(1)}, bf16[2064,128]{1,0:T(8,128)(2,1)S(1)}, u32[]{:S(2)}, u32[]{:S(2)}) collective-permute-start(bf16[2064,128]{1,0:T(8,128)(2,1)S(1)} %get-tuple-element.19.after_ref), channel_id=1, source_target_pairs={{32,64},{96,128},{160,192},{224,256},{288,320},{352,384},{416,448}... | collective-permute-start | bytes 1585160 | tf_op jit(solution)/shard_map/ppermute | solution.py:359
  3.8 5.7 %copy-start.2 = (s32[65536,1]{0,1:T(1,128)S(1)}, s32[65536,1]{0,1:T(1,128)}, u32[]{:S(2)}) copy-start(s32[65536,1]{0,1:T(1,128)} %param.11) | copy-start | bytes 786436
  3.8 5.7 %copy-start.3 = (s32[65536]{0:T(1024)S(1)}, s32[65536]{0:T(1024)}, u32[]{:S(2)}) copy-start(s32[65536]{0:T(1024)} %param.12) | copy-start | bytes 786436
  3.8 5.7 %copy-start.4 = (s32[2048,3]{0,1:T(4,128)S(1)}, s32[2048,3]{0,1:T(4,128)}, u32[]{:S(2)}) copy-start(s32[2048,3]{0,1:T(4,128)} %param.10) | copy-start | bytes 73732
  3.8 5.7 %copy-start.5 = (f32[16]{0:T(128)S(1)}, f32[16]{0:T(128)}, u32[]{:S(2)}) copy-start(f32[16]{0:T(128)} %param.9) | copy-start | bytes 196
  3.8 5.7 %copy-start.6 = (s32[5]{0:T(128)S(1)}, s32[5]{0:T(128)}, u32[]{:S(2)}) copy-start(s32[5]{0:T(128)} %param.13) | copy-start | bytes 64
  5.3 6.6 %collective-permute-start.1 = (bf16[2064,128]{1,0:T(8,128)(2,1)S(1)}, bf16[2064,128]{1,0:T(8,128)(2,1)S(1)}, u32[]{:S(2)}, u32[]{:S(2)}) collective-permute-start(bf16[2064,128]{1,0:T(8,128)(2,1)S(1)} %get-tuple-element.28), channel_id=1, source_target_pairs={{0,32},{32,0},{64,96},{96,64},{128,160},{160,128},{192,224},{224,1... | collective-permute-start | bytes 1585160 | tf_op jit(solution)/shard_map/ppermute | solution.py:361

commit v6 on v5

--- a/solution.py
+++ b/solution.py
@@ -382,7 +382,7 @@
     )
     parts = window(
         far_kernel, "far_window", jax.ShapeDtypeStruct((chan_count, pitch, LANES), BF16),
-        [pltpu.VMEM((chan_count * pitch, LANES), F32)], work,
+        [pltpu.VMEM(((chan_count + 1) * pitch, LANES), F32)], work,
         (far_strip, far_taps, gains, onehot, others, own),
     )
     parts = lax.all_to_all(parts, "chan", split_axis=0, concat_axis=0, tiled=True)

time: 38.1 us -> 38.1 us (level)
  no operation moved by 1% of the time
where the time goes in v6:
time: 38.1 us; the launch traced here: 37.9 us
  blocking collectives  21.5 us (56%)
  Pallas kernels  9.81 us (26%)
  starting transfers between devices  6.38 us (17%)
    all_to_all x1, blocking collectives, shards(): lax.all_to_all(parts, 'chan', split_axis=0, concat_axis=0, tiled=True)  21.5 us
    pallas_call x3, Pallas kernels, window(): pl.pallas_call(kernel, in_specs=[vmem] * len(args), out_specs=[vmem] * le...  6.17 us
    ppermute x1, starting transfers between devices, shards(): near_strip = lax.ppermute(near_sent, 'tm', near_pairs)  4.15 us
    ppermute x1, starting transfers between devices, shards(): far_strip = lax.ppermute(far_sent, 'tm', far_pairs)  2.24 us
    pallas_call x1, Pallas kernels, near_pack(): pl.pallas_call(near_pack_kernel, in_specs=[vmem, pl.BlockSpec(memory_spac...  1.51 us
    pallas_call x1, Pallas kernels, first(): pl.pallas_call(first_kernel, in_specs=[pl.BlockSpec(memory_space=pltpu.HB...  1.47 us
  transfers between devices with their start and end apart: 2, of which 0 were waited for; matrix products, arithmetic and copies ran while one was open for 0% of the time, Pallas kernels for 17%

profile of v6, /device:TPU:192, one launch (start us, length us, event | category | flops | bytes accessed | tf_op | source)
XLA Modules:
  0.0 37.9 jit_solution(7529818778382027416)
XLA Ops:
  0.0 0.0 copy-start
  0.0 0.0 copy-start.1
  0.0 1.5 %far_strip.1 = (bf16[2064,128]{1,0:T(8,128)(2,1)S(1)}, bf16[768,512]{1,0:T(8,128)(2,1)S(1)}, bf16[432,512]{1,0:T(8,128)(2,1)S(1)}, bf16[432,512]{1,0:T(8,128)(2,1)S(1)}) custom-call(bf16[2048,512]{1,0:T(8,128)(2,1)} %raw_ref.7, f32[3,257]{1,0:T(4,128)} %taps_ref.5), custom_call_target="tpu_custom_call" | custom-call | tf_op jit(solution)/shard_map/far_strip/pallas_call | solution.py:85
  1.5 2.2 %collective-permute-start = (bf16[2064,128]{1,0:T(8,128)(2,1)S(1)}, bf16[2064,128]{1,0:T(8,128)(2,1)S(1)}, u32[]{:S(2)}, u32[]{:S(2)}) collective-permute-start(bf16[2064,128]{1,0:T(8,128)(2,1)S(1)} %get-tuple-element.19.after_ref), channel_id=1, source_target_pairs={{32,64},{96,128},{160,192},{224,256},{288,320},{352,384},{416,448}... | collective-permute-start | bytes 1585160 | tf_op jit(solution)/shard_map/ppermute | solution.py:359
  3.7 0.0 copy-done
  3.7 0.0 copy-done.1
  3.8 0.0 copy-start.2
  3.8 0.0 copy-start.3
  3.8 0.0 copy-start.4
  3.8 0.0 copy-start.5
  3.8 0.0 copy-start.6
  3.8 1.5 %near_strip.1 = (bf16[2064,128]{1,0:T(8,128)(2,1)S(1)}, bf16[768,512]{1,0:T(8,128)(2,1)S(1)}, bf16[432,512]{1,0:T(8,128)(2,1)S(1)}, bf16[432,512]{1,0:T(8,128)(2,1)S(1)}) custom-call(bf16[2048,512]{1,0:T(8,128)(2,1)S(1)} %copy-done, bf16[2064,128]{1,0:T(8,128)(2,1)S(1)} %get-tuple-element.19.after_ref, f32[3,257]{1,0:T(4,128)S(1)} %copy-done.1, ...), custom_call_target="tpu_custom_call" | custom-call | flops 1610612736 | bytes 4194304 | tf_op jit(solution)/shard_map/near_strip/pallas_call | solution.py:103
  5.3 4.1 %collective-permute-start.1 = (bf16[2064,128]{1,0:T(8,128)(2,1)S(1)}, bf16[2064,128]{1,0:T(8,128)(2,1)S(1)}, u32[]{:S(2)}, u32[]{:S(2)}) collective-permute-start(bf16[2064,128]{1,0:T(8,128)(2,1)S(1)} %get-tuple-element.28), channel_id=1, source_target_pairs={{0,32},{32,0},{64,96},{96,64},{128,160},{160,128},{192,224},{224,1... | collective-permute-start | bytes 1585160 | tf_op jit(solution)/shard_map/ppermute | solution.py:361
  9.5 0.0 copy-done.2
  9.5 0.0 copy-done.3
  9.5 0.0 copy-done.4
  9.5 0.0 copy-done.5
  9.5 0.0 copy-done.6
  9.5 2.4 %inner_window.1 = (f32[160,256]{1,0:T(8,128)S(1)}, f32[8,2048]{1,0:T(8,128)S(1)}, bf16[160,2048]{1,0:T(8,128)(2,1)S(1)}, f32[24,128]{1,0:T(8,128)S(1)}) custom-call(f32[1,16]{1,0:T(1,128)S(1)} %bitcast.8, s32[1,5]{1,0:T(1,128)S(1)} %bitcast.9, bf16[2048,512]{1,0:T(8,128)(2,1)S(1)} %copy-done, bf16[768,512]{1,0:T(8,128)(2,1)S(1)} %get-tuple-element.23.inner_taps_ref, ...), custom_call_target="tpu_custom_call" | custom-call | flops 80530636800 | bytes 4194304 | tf_op jit(solution)/shard_map/inner_window/pallas_call | solution.py:314
  12.0 0.0 collective-permute-done.1.strip_ref
  12.0 2.6 %near_window.1 = (f32[160,512]{1,0:T(8,128)S(1)}, f32[144,2048]{1,0:T(8,128)S(1)}) custom-call(bf16[2048,512]{1,0:T(8,128)(2,1)S(1)} %copy-done, bf16[2064,128]{1,0:T(8,128)(2,1)S(1)} %collective-permute-done.1.strip_ref, bf16[432,512]{1,0:T(8,128)(2,1)S(1)} %get-tuple-element.29.taps_ref, f32[8,2048]{1,0:T(8,128)S(1)} %get-tuple-element.26.gains_ref, ...), custom_call_target="tpu_custom_call" | custom-call | flops 1610612736 | bytes 4194304 | tf_op jit(solution)/shard_map/near_window/pallas_call | solution.py:314
  14.6 0.0 collective-permute-done.strip_ref
  14.6 1.2 %far_window.1 = bf16[32,24,128]{2,1,0:T(8,128)(2,1)S(1)} custom-call(bf16[2064,128]{1,0:T(8,128)(2,1)S(1)} %collective-permute-done.strip_ref, bf16[432,512]{1,0:T(8,128)(2,1)S(1)} %get-tuple-element.25.far_taps_ref.taps_ref, f32[8,2048]{1,0:T(8,128)S(1)} %get-tuple-element.26.gains_ref, bf16[160,2048]{1,0:T(8,128)(2,1)S(1)} %get-tuple-element.27.onehot_ref, ...), custom_call_target="tpu_custom_call" | custom-call | flops 1610612736 | bytes 4194304 | tf_op jit(solution)/shard_map/far_window/pallas_call | solution.py:314
  15.7 21.5 %all_to_all.5.parts_ref = bf16[32,24,128]{2,1,0:T(8,128)(2,1)S(1)} all-to-all(bf16[32,24,128]{2,1,0:T(8,128)(2,1)S(1)} %far_window.1), channel_id=1, replica_groups=mesh['tm'=16,'chan'=32] {'chan'}, dimensions={0} | all-to-all | bytes 393216 | tf_op jit(solution)/shard_map/all_to_all | solution.py:388
  37.3 0.7 %finish_sum.1 = f32[5,512]{1,0:T(8,128)} custom-call(f32[24,128]{1,0:T(8,128)S(1)} %get-tuple-element.24.divisor_ref, bf16[32,24,128]{2,1,0:T(8,128)(2,1)S(1)} %all_to_all.5.parts_ref), custom_call_target="tpu_custom_call" | custom-call | tf_op jit(solution)/shard_map/finish_sum/pallas_call | solution.py:338
Async XLA Ops:
  0.0 3.7 %copy-start = (bf16[2048,512]{1,0:T(8,128)(2,1)S(1)}, bf16[2048,512]{1,0:T(8,128)(2,1)}, u32[]{:S(2)}) copy-start(bf16[2048,512]{1,0:T(8,128)(2,1)} %raw_ref.7) | copy-start | bytes 6291460
  0.0 3.7 %copy-start.1 = (f32[3,257]{1,0:T(4,128)S(1)}, f32[3,257]{1,0:T(4,128)}, u32[]{:S(2)}) copy-start(f32[3,257]{1,0:T(4,128)} %taps_ref.5) | copy-start | bytes 9256
  1.5 13.1 %collective-permute-start = (bf16[2064,128]{1,0:T(8,128)(2,1)S(1)}, bf16[2064,128]{1,0:T(8,128)(2,1)S(1)}, u32[]{:S(2)}, u32[]{:S(2)}) collective-permute-start(bf16[2064,128]{1,0:T(8,128)(2,1)S(1)} %get-tuple-element.19.after_ref), channel_id=1, source_target_pairs={{32,64},{96,128},{160,192},{224,256},{288,320},{352,384},{416,448}... | collective-permute-start | bytes 1585160 | tf_op jit(solution)/shard_map/ppermute | solution.py:359
  3.8 5.7 %copy-start.2 = (s32[65536,1]{0,1:T(1,128)S(1)}, s32[65536,1]{0,1:T(1,128)}, u32[]{:S(2)}) copy-start(s32[65536,1]{0,1:T(1,128)} %param.11) | copy-start | bytes 786436
  3.8 5.7 %copy-start.3 = (s32[65536]{0:T(1024)S(1)}, s32[65536]{0:T(1024)}, u32[]{:S(2)}) copy-start(s32[65536]{0:T(1024)} %param.12) | copy-start | bytes 786436
  3.8 5.7 %copy-start.4 = (s32[2048,3]{0,1:T(4,128)S(1)}, s32[2048,3]{0,1:T(4,128)}, u32[]{:S(2)}) copy-start(s32[2048,3]{0,1:T(4,128)} %param.10) | copy-start | bytes 73732
  3.8 5.7 %copy-start.5 = (f32[16]{0:T(128)S(1)}, f32[16]{0:T(128)}, u32[]{:S(2)}) copy-start(f32[16]{0:T(128)} %param.9) | copy-start | bytes 196
  3.8 5.7 %copy-start.6 = (s32[5]{0:T(128)S(1)}, s32[5]{0:T(128)}, u32[]{:S(2)}) copy-start(s32[5]{0:T(128)} %param.13) | copy-start | bytes 64
  5.3 6.6 %collective-permute-start.1 = (bf16[2064,128]{1,0:T(8,128)(2,1)S(1)}, bf16[2064,128]{1,0:T(8,128)(2,1)S(1)}, u32[]{:S(2)}, u32[]{:S(2)}) collective-permute-start(bf16[2064,128]{1,0:T(8,128)(2,1)S(1)} %get-tuple-element.28), channel_id=1, source_target_pairs={{0,32},{32,0},{64,96},{96,64},{128,160},{160,128},{192,224},{224,1... | collective-permute-start | bytes 1585160 | tf_op jit(solution)/shard_map/ppermute | solution.py:361
